TPU v7x, 512 devices: a whole 4x8x8 slice. The times are simulated.
512 devices in a mesh: owner: 64 (over x, z, core), kv: 8 (over y).
Axes of the slice: x: 4, y: 8, z: 8, core: 2. Of those that a mesh axis runs over, the one named last changes fastest.
Arguments:
- queries: bfloat16 [2048, 8192], P(('owner', 'kv')), may hold values from -30 to 30
- paths: int32 [2048, 3], P('owner'), may hold values from 0 to 63, all different within a row; in each aligned block of 32 rows (0 to 31, 32 to 63, ...) at most 8 rows name the same one
- node_owner: int32 [64], replicated, may hold values from 0 to 63, each once
- node_len: int32 [64], replicated, may hold values from 1 to 512, 8192 in all
- suf_len: int32 [2048], P('owner'), may hold values from 1 to 64, 65536 in all
- prefix_kv: bfloat16 [64, 2, 512, 1024], P('owner', None, None, 'kv'), may hold values from -30 to 30
- suffix_key_value: bfloat16 [2048, 2, 64, 1024], P('owner', None, None, 'kv'), may hold values from -30 to 30
- fresh_key_value: bfloat16 [2048, 2, 1024], P('owner', None, 'kv'), may hold values from -30 to 30
Outputs:
- attended: bfloat16 [2048, 8192], P(('owner', 'kv'))
Inputs may be any that keep to these rules, and one draw needn't show every extreme that they name: `paths`: the 3 nodes of a request are distinct. Among the 32 requests of one owner index (aligned blocks of rows), no node is named by more than 8 of them, a bound that some block reaches.
All inputs are finite; a program needn't handle non-finite values. No bound on the sum of `suf_len` on one device may be relied on, other than what follows from the above.
Results may differ from a plain program's by a relative error of at most 0.0022.
Values may be sent and summed in bfloat16 or wider, within the bound.
No kernel may reach another device: no remote copies, remote signals or barrier semaphores. Data moves between devices by JAX's collectives and lax.ppermute only.
A program may use at most 64 MiB of HBM per device.

v0:
```python
import jax
import jax.numpy as jnp
from jax import lax
from jax.sharding import PartitionSpec as P

QUERY_HEADS = 64
KEY_VALUE_HEADS = 8
HEAD_SIZE = 128
PATH = 3


def attend_shared(query_head_rows, key_matrix, value_matrix, length):
    scores = jnp.einsum(
        "mkgd,tkd->mkgt", query_head_rows, key_matrix, preferred_element_type=jnp.float32
    ) * HEAD_SIZE ** (-0.5)
    validity_mask = lax.iota(jnp.int32, key_matrix.shape[0]) < length
    highest = jnp.max(jnp.where(validity_mask, scores, -jnp.inf), axis=-1)
    weights = jnp.where(validity_mask, jnp.exp(scores - highest[..., None]), 0.0)
    weight_sum = jnp.sum(weights, axis=-1)
    summed = jnp.einsum(
        "mkgt,tkd->mkgd",
        weights.astype(jnp.bfloat16),
        value_matrix,
        preferred_element_type=jnp.float32,
    )
    return (highest, weight_sum, summed)


def shards(
    queries, paths, node_owner, node_len, suf_len, prefix_kv, suffix_key_value, fresh_key_value
):
    owners = lax.axis_size("owner")
    kv_index = lax.axis_index("kv")
    request_count = paths.shape[0]
    heads_kv = prefix_kv.shape[-1] // HEAD_SIZE
    query_head_group = QUERY_HEADS // KEY_VALUE_HEADS
    heads_local = heads_kv * query_head_group
    width_local = heads_local * HEAD_SIZE
    all_queries = lax.all_gather(queries, "kv", axis=0, tiled=True)
    local_queries = lax.dynamic_slice_in_dim(all_queries, kv_index * width_local, width_local, 1)
    query_head_rows = local_queries.reshape(request_count, heads_kv, query_head_group, HEAD_SIZE)
    node_ids = lax.iota(jnp.int32, node_owner.shape[0])
    holders = jnp.sum(
        jnp.where(paths[:, :, None] == node_ids[None, None, :], node_owner[None, None, :], 0),
        axis=-1,
    )
    capacity = min(request_count, max(8, 2 * request_count * PATH // owners))
    flat_dest = holders.reshape(-1)
    dest_table = (flat_dest[:, None] == lax.iota(jnp.int32, owners)[None, :]).astype(jnp.int32)
    earlier = jnp.cumsum(dest_table, axis=0) - dest_table
    rank_index = jnp.sum(earlier * dest_table, axis=1)
    slot_index = flat_dest * capacity + rank_index
    sent_queries = jnp.repeat(local_queries, PATH, axis=0)
    outgoing = (
        jnp.zeros((owners * capacity, width_local), jnp.bfloat16).at[slot_index].set(sent_queries)
    )
    own_length = jnp.sum(jnp.where(node_ids == lax.axis_index("owner"), node_len, 0))
    own_keys = prefix_kv[0, 0].reshape(-1, heads_kv, HEAD_SIZE)
    own_values = prefix_kv[0, 1].reshape(-1, heads_kv, HEAD_SIZE)
    received = lax.all_to_all(
        outgoing.reshape(owners, capacity, width_local),
        "owner",
        split_axis=0,
        concat_axis=0,
        tiled=True,
    )
    sources = received.shape[0]
    slot_count = received.shape[1]
    total_slots = sources * slot_count
    slot_heads = received.reshape(total_slots, heads_kv, query_head_group, HEAD_SIZE)
    block_rows = max(1, 512 // heads_local)
    block_count = -(-total_slots // block_rows)

    def one_block(block_heads):
        return attend_shared(block_heads, own_keys, own_values, own_length)

    highs, sums, outputs = lax.map(
        one_block,
        slot_heads.reshape(block_count, block_rows, heads_kv, query_head_group, HEAD_SIZE),
    )
    highs = highs.reshape(block_count * block_rows, heads_local).reshape(
        sources, slot_count, heads_local
    )
    sums = sums.reshape(block_count * block_rows, heads_local).reshape(
        sources, slot_count, heads_local
    )
    outputs = outputs.reshape(block_count * block_rows, width_local).reshape(
        sources, slot_count, width_local
    )
    back_out = lax.all_to_all(outputs, "owner", split_axis=0, concat_axis=0, tiled=True)
    back_high = lax.all_to_all(highs, "owner", split_axis=0, concat_axis=0, tiled=True)
    back_sum = lax.all_to_all(sums, "owner", split_axis=0, concat_axis=0, tiled=True)
    prefix_out = back_out.reshape(owners * capacity, width_local)[slot_index].reshape(
        request_count, PATH, heads_local, HEAD_SIZE
    )
    prefix_high = back_high.reshape(owners * capacity, heads_local)[slot_index].reshape(
        request_count, PATH, heads_local
    )
    prefix_sum = back_sum.reshape(owners * capacity, heads_local)[slot_index].reshape(
        request_count, PATH, heads_local
    )
    suffix_keys = suffix_key_value[:, 0].reshape(request_count, -1, heads_kv, HEAD_SIZE)
    suffix_values = suffix_key_value[:, 1].reshape(request_count, -1, heads_kv, HEAD_SIZE)
    newest_keys = fresh_key_value[:, 0].reshape(request_count, heads_kv, HEAD_SIZE)
    newest_values = fresh_key_value[:, 1].reshape(request_count, heads_kv, HEAD_SIZE)
    suffix_scores = jnp.einsum(
        "rkgd,rtkd->rkgt", query_head_rows, suffix_keys, preferred_element_type=jnp.float32
    ) * HEAD_SIZE ** (-0.5)
    newest_scores = jnp.einsum(
        "rkgd,rkd->rkg", query_head_rows, newest_keys, preferred_element_type=jnp.float32
    ) * HEAD_SIZE ** (-0.5)
    suffix_valid = (lax.iota(jnp.int32, suffix_keys.shape[1])[None, :] < suf_len[:, None])[
        :, None, None, :
    ]
    local_high = jnp.maximum(
        jnp.max(jnp.where(suffix_valid, suffix_scores, -jnp.inf), axis=-1), newest_scores
    )
    suffix_weights = jnp.where(suffix_valid, jnp.exp(suffix_scores - local_high[..., None]), 0.0)
    newest_weight = jnp.exp(newest_scores - local_high)
    local_sum = jnp.sum(suffix_weights, axis=-1) + newest_weight
    local_out = jnp.einsum(
        "rkgt,rtkd->rkgd",
        suffix_weights.astype(jnp.bfloat16),
        suffix_values,
        preferred_element_type=jnp.float32,
    )
    local_out = (
        local_out
        + newest_weight.astype(jnp.bfloat16).astype(jnp.float32)[..., None]
        * newest_values.astype(jnp.float32)[:, :, None, :]
    )
    every_high = jnp.concatenate([prefix_high, local_high], axis=1)
    every_sum = jnp.concatenate([prefix_sum, local_sum], axis=1)
    every_out = jnp.concatenate([prefix_out, local_out], axis=1)
    best = jnp.max(every_high, axis=1, keepdims=True)
    factors = jnp.exp(every_high - best)
    numer = jnp.sum(factors[..., None] * every_out, axis=1)
    denom = jnp.sum(factors * every_sum, axis=1)
    attended = (numer / denom[..., None]).reshape(request_count, width_local).astype(jnp.bfloat16)
    full_heads = lax.all_gather(attended, "kv", axis=1, tiled=True)
    rows_each = request_count // lax.axis_size("kv")
    return lax.dynamic_slice_in_dim(full_heads, kv_index * rows_each, rows_each, 0)


def solution(mesh):
    return jax.shard_map(
        shards,
        mesh=mesh,
        in_specs=(
            P(("owner", "kv"), None),
            P("owner", None),
            P(),
            P(),
            P("owner"),
            P("owner", None, None, "kv"),
            P("owner", None, None, "kv"),
            P("owner", None, "kv"),
        ),
        out_specs=P(("owner", "kv"), None),
        check_vma=False,
    )
```

profile of v0, /device:TPU:16, one launch (start us, length us, event | category | flops | bytes accessed | tf_op | source)
XLA Modules:
  0.0 218.8 jit_solution(14352889760174577594)
XLA Ops:
  1.7 28.9 %all-gather = bf16[8,4,8192]{2,1,0:T(4,128)(2,1)S(1)} all-gather(bf16[1,4,8192]{2,1,0:T(4,128)(2,1)} %bitcast.136), channel_id=1, replica_groups=mesh['owner'=64,'kv'=8] {'kv'}, dimensions={0}, use_global_device_ids=true | all-gather | bytes 589824 | tf_op jit(solution)/shard_map/all_gather | solution.py:39
  31.0 2.1 scatter_custom_fusion
  33.2 11.8 %all-to-all-start = ((bf16[64,8,1024]{2,1,0:T(8,128)(2,1)}), bf16[64,8,1024]{2,1,0:T(8,128)(2,1)S(1)}, u32[]{:S(2)}, u32[]{:S(2)}) async-start(bf16[64,8,1024]{2,1,0:T(8,128)(2,1)} %bitcast.19), calls=%async_computation | async-start | bytes 2097152 | tf_op jit(solution)/shard_map/all_to_all | solution.py:60
  45.6 27.5 %all-to-all-done = bf16[64,8,1024]{2,1,0:T(8,128)(2,1)S(1)} async-done(((bf16[64,8,1024]{2,1,0:T(8,128)(2,1)}), bf16[64,8,1024]{2,1,0:T(8,128)(2,1)S(1)}, u32[]{:S(2)}, u32[]{:S(2)}) %all-to-all-start) | async-done | bytes 1048608 | tf_op jit(solution)/shard_map/all_to_all | solution.py:60
  73.4 23.6 %while.14 = (s32[]{:T(128)}, f32[8,64,1,8]{3,1,2,0:T(8,128)}, f32[8,64,1,8]{3,1,2,0:T(8,128)S(1)}, f32[8,64,1,8,128]{4,3,1,2,0:T(8,128)}, s32[]{:T(128)}, /*inde...) while((s32[]{:T(128)}, f32[8,64,1,8]{3,1,2,0:T(8,128)}, ...), condition=%wide.region_8.9_spmd, body=%wide.region_5.8_spmd.sunk | while | flops 136576512 | bytes 3942517 | solution.py:77
  75.3 1.1 fusion.46
  84.1 1.1 fusion.46
  87.1 1.1 fusion.46
  90.0 1.1 fusion.46
  95.9 1.1 fusion.46
  97.0 6.6 %all-to-all-start.1 = ((f32[64,8,8]{2,1,0:T(8,128)}), f32[64,8,8]{2,1,0:T(8,128)S(1)}, u32[]{:S(2)}, u32[]{:S(2)}) async-start(f32[64,8,8]{2,1,0:T(8,128)} %bitcast.22), calls=%async_computation.1 | async-start | bytes 524288 | tf_op jit(solution)/shard_map/all_to_all | solution.py:91
  104.4 11.2 %all-to-all-done.1 = f32[64,8,8]{2,1,0:T(8,128)S(1)} async-done(((f32[64,8,8]{2,1,0:T(8,128)}), f32[64,8,8]{2,1,0:T(8,128)S(1)}, u32[]{:S(2)}, u32[]{:S(2)}) %all-to-all-start.1) | async-done | bytes 16416 | tf_op jit(solution)/shard_map/all_to_all | solution.py:91
  115.5 6.0 %all-to-all-start.3 = ((f32[64,8,8]{1,2,0:T(8,128)}), f32[64,8,8]{1,2,0:T(8,128)S(1)}, u32[]{:S(2)}, u32[]{:S(2)}) async-start(f32[64,8,8]{1,2,0:T(8,128)} %copy.64), calls=%async_computation.3 | async-start | bytes 524288 | tf_op jit(solution)/shard_map/all_to_all | solution.py:92
  121.6 2.7 %reshape_reshape.14 = f32[64,8,1024]{2,1,0:T(8,128)} reshape(f32[8,64,1,8,128]{4,3,1,2,0:T(8,128)} %get-tuple-element.50) | data formatting | bytes 4194304 | tf_op jit(solution)/shard_map/reshape;reshape | solution.py:87
  124.3 9.2 %all-to-all-done.3 = f32[64,8,8]{1,2,0:T(8,128)S(1)} async-done(((f32[64,8,8]{1,2,0:T(8,128)}), f32[64,8,8]{1,2,0:T(8,128)S(1)}, u32[]{:S(2)}, u32[]{:S(2)}) %all-to-all-start.3) | async-done | bytes 16416 | tf_op jit(solution)/shard_map/all_to_all | solution.py:92
  134.3 6.0 %all-to-all-start.2 = ((f32[64,8,1024]{2,1,0:T(8,128)}), f32[64,8,1024]{2,1,0:T(8,128)S(1)}, u32[]{:S(2)}, u32[]{:S(2)}) async-start(f32[64,8,1024]{2,1,0:T(8,128)} %reshape_reshape.14), calls=%async_computation.2 | async-start | bytes 4194304 | tf_op jit(solution)/shard_map/all_to_all | solution.py:90
  143.3 1.9 select_reduce_fusion.1
  145.2 1.2 gather_fusion
  150.9 1.3 add_bitcast_fusion
  152.9 1.1 copy.65
  154.0 1.3 gather_fusion.2
  157.1 1.1 fusion.13
  158.2 33.3 %all-to-all-done.2 = f32[64,8,1024]{2,1,0:T(8,128)S(1)} async-done(((f32[64,8,1024]{2,1,0:T(8,128)}), f32[64,8,1024]{2,1,0:T(8,128)S(1)}, u32[]{:S(2)}, u32[]{:S(2)}) %all-to-all-start.2) | async-done | bytes 2097184 | tf_op jit(solution)/shard_map/all_to_all | solution.py:90
  192.8 25.3 %all_gather.7 = bf16[32,8192]{1,0:T(8,128)(2,1)S(1)} all-gather(bf16[32,1024]{1,0:T(8,128)(2,1)S(1)} %bitcast.133), channel_id=1, replica_groups=mesh['owner'=64,'kv'=8] {'kv'}, dimensions={1}, use_global_device_ids=true | all-gather | bytes 589824 | tf_op jit(solution)/shard_map/all_gather | solution.py:140
  (104 shorter events, 34.4 us)
Async XLA Ops:
  30.7 14.9 %copy-start.2 = (bf16[32,8192]{1,0:T(8,128)(2,1)}, bf16[32,8192]{1,0:T(8,128)(2,1)S(1)}, u32[]{:S(2)}) copy-start(bf16[32,8192]{1,0:T(8,128)(2,1)S(1)} %reshape.229) | copy-start | bytes 1572868
  30.7 14.2 %copy-start.10 = (s32[64]{0:T(128)S(1)}, s32[64]{0:T(128)}, u32[]{:S(2)}) copy-start(s32[64]{0:T(128)} %param.13) | copy-start | bytes 772
  30.7 14.8 %copy-start.4 = (bf16[1,2,512,128]{3,2,1,0:T(8,128)(2,1)S(1)}, bf16[1,2,512,128]{3,2,1,0:T(8,128)(2,1)}, u32[]{:S(2)}) copy-start(bf16[1,2,512,128]{3,2,1,0:T(8,128)(2,1)} %param.15) | copy-start | bytes 786436
  31.0 42.1 %copy-start.9 = (s32[96]{0:T(128)}, s32[96]{0:T(128)S(1)}, u32[]{:S(2)}) copy-start(s32[96]{0:T(128)S(1)} %fusion.33) | copy-start | bytes 1156
  33.2 39.9 %all-to-all-start = ((bf16[64,8,1024]{2,1,0:T(8,128)(2,1)}), bf16[64,8,1024]{2,1,0:T(8,128)(2,1)S(1)}, u32[]{:S(2)}, u32[]{:S(2)}) async-start(bf16[64,8,1024]{2,1,0:T(8,128)(2,1)} %bitcast.19), calls=%async_computation | async-start | bytes 2097152 | tf_op jit(solution)/shard_map/all_to_all | solution.py:60
  97.0 18.6 %all-to-all-start.1 = ((f32[64,8,8]{2,1,0:T(8,128)}), f32[64,8,8]{2,1,0:T(8,128)S(1)}, u32[]{:S(2)}, u32[]{:S(2)}) async-start(f32[64,8,8]{2,1,0:T(8,128)} %bitcast.22), calls=%async_computation.1 | async-start | bytes 524288 | tf_op jit(solution)/shard_map/all_to_all | solution.py:91
  115.5 18.0 %all-to-all-start.3 = ((f32[64,8,8]{1,2,0:T(8,128)}), f32[64,8,8]{1,2,0:T(8,128)S(1)}, u32[]{:S(2)}, u32[]{:S(2)}) async-start(f32[64,8,8]{1,2,0:T(8,128)} %copy.64), calls=%async_computation.3 | async-start | bytes 524288 | tf_op jit(solution)/shard_map/all_to_all | solution.py:92
  124.3 16.0 %copy-start.6 = (bf16[32,2,128]{2,1,0:T(2,128)(2,1)S(1)}, bf16[32,2,128]{2,1,0:T(2,128)(2,1)}, u32[]{:S(2)}) copy-start(bf16[32,2,128]{2,1,0:T(2,128)(2,1)} %param.17) | copy-start | bytes 49156
  124.3 18.1 %copy-start.8 = (s32[32]{0:T(128)S(1)}, s32[32]{0:T(128)}, u32[]{:S(2)}) copy-start(s32[32]{0:T(128)} %param.14) | copy-start | bytes 388
  124.3 19.0 %copy-start = (bf16[32,2,64,128]{3,2,1,0:T(8,128)(2,1)S(1)}, bf16[32,2,64,128]{3,2,1,0:T(8,128)(2,1)}, u32[]{:S(2)}) copy-start(bf16[32,2,64,128]{3,2,1,0:T(8,128)(2,1)} %param.16) | copy-start | bytes 3145732
  133.6 0.7 copy-start.1
  134.3 57.2 %all-to-all-start.2 = ((f32[64,8,1024]{2,1,0:T(8,128)}), f32[64,8,1024]{2,1,0:T(8,128)S(1)}, u32[]{:S(2)}, u32[]{:S(2)}) async-start(f32[64,8,1024]{2,1,0:T(8,128)} %reshape_reshape.14), calls=%async_computation.2 | async-start | bytes 4194304 | tf_op jit(solution)/shard_map/all_to_all | solution.py:90
  141.8 0.7 copy-start.3
  142.5 5.5 %copy-start.7 = (s32[1024]{0:T(1024)}, s32[1024]{0:T(1024)S(1)}, u32[]{:S(2)}) copy-start(s32[1024]{0:T(1024)S(1)} %pad_clamp_fusion) | copy-start | bytes 12292
  142.5 0.8 copy-start.5
where the time goes:
time: 220 us; the launch traced here: 219 us
  waiting for transfers between devices  81.2 us (37%)
  blocking collectives  54.2 us (25%)
  starting transfers between devices  30.4 us (14%)
  local copies, waits for them, and re-layouts  23.1 us (10%)
  matrix products  15.3 us (7%)
  other arithmetic  14.2 us (6%)
    all_to_all x1, waiting for transfers between devices, shards(): lax.all_to_all(outputs, 'owner', split_axis=0, concat_axis=0, tiled=True)  33.3 us
    all_gather x1, blocking collectives, shards(): all_queries = lax.all_gather(queries, 'kv', axis=0, tiled=True)  28.9 us
    all_to_all x1, waiting for transfers between devices, shards(): lax.all_to_all(outgoing.reshape(owners, capacity, width_local), 'owner',...  27.5 us
    all_gather x1, blocking collectives, shards(): full_heads = lax.all_gather(attended, 'kv', axis=1, tiled=True)  25.3 us
    all_to_all x1, starting transfers between devices, shards(): lax.all_to_all(outgoing.reshape(owners, capacity, width_local), 'owner',...  11.8 us
    all_to_all x1, waiting for transfers between devices, shards(): lax.all_to_all(highs, 'owner', split_axis=0, concat_axis=0, tiled=True)  11.2 us
    all_to_all x1, waiting for transfers between devices, shards(): lax.all_to_all(sums, 'owner', split_axis=0, concat_axis=0, tiled=True)  9.24 us
    dot_general x8, matrix products, attend_shared(): jnp.einsum('mkgt,tkd->mkgd', weights.astype(jnp.bfloat16), value_matrix,...  8.48 us
  transfers between devices with their start and end apart: 4, of which 4 were waited for; matrix products, arithmetic and copies ran while one was open for 10% of the time, Pallas kernels for 0%

commit v1 on v0

v1 whole, which is shorter than its diff:
```python
import jax
import jax.numpy as jnp
from jax import lax
from jax.experimental import pallas as pl
from jax.experimental.pallas import tpu as pltpu
from jax.sharding import Mesh
from jax.sharding import PartitionSpec as P

QUERY_HEADS = 64
KEY_VALUE_HEADS = 8
HEAD_SIZE = 128
PATH = 3
GROUP = QUERY_HEADS // KEY_VALUE_HEADS
WIDTH = GROUP * HEAD_SIZE
PAD_WIDTH = WIDTH + 128
SCALE = HEAD_SIZE ** (-0.5)
LOW = -1e30
SLOTS = 32
TILE = 8
AXES = ("x", "zh", "zl", "core", "kv")
OWNER = ("x", "zh", "zl", "core")


def nt(a, b):
    return lax.dot_general(a, b, (((1,), (1,)), ((), ())), preferred_element_type=jnp.float32)


def spread_heads(rows_ref, heads_ref):
    count = rows_ref.shape[0]
    for head in range(GROUP):
        part = rows_ref[:, head * HEAD_SIZE : (head + 1) * HEAD_SIZE].astype(jnp.float32)
        heads_ref[pl.ds(head, count, stride=GROUP), :] = part


def suffix_kernel(query_ref, cache_ref, fresh_ref, valid_ref, out_ref, high_ref, sum_ref, heads_ref):
    spread_heads(query_ref, heads_ref)
    requests, _, length, _ = cache_ref.shape
    block = 8
    rows = block * GROUP
    row_request = lax.broadcasted_iota(jnp.int32, (rows, 1), 0) // GROUP
    key_request = lax.broadcasted_iota(jnp.int32, (1, block * length), 1) // length
    fresh_request = lax.broadcasted_iota(jnp.int32, (1, requests), 1)
    own_key = row_request == key_request
    for group in range(requests // block):
        here = pl.ds(group * rows, rows)
        query = heads_ref[here, :].astype(jnp.bfloat16)
        keys = cache_ref[group * block : (group + 1) * block, 0].reshape(block * length, HEAD_SIZE)
        values = cache_ref[group * block : (group + 1) * block, 1].reshape(block * length, HEAD_SIZE)
        usable = own_key & (valid_ref[group : group + 1, :] > 0)
        scores = jnp.where(usable, nt(query, keys) * SCALE, LOW)
        newest = jnp.where(
            fresh_request == row_request + group * block, nt(query, fresh_ref[0]) * SCALE, LOW
        )
        high = jnp.maximum(
            jnp.max(scores, axis=1, keepdims=True), jnp.max(newest, axis=1, keepdims=True)
        )
        weights = jnp.exp(scores - high)
        newest_weights = jnp.exp(newest - high)
        total = jnp.sum(weights, axis=1, keepdims=True) + jnp.sum(
            newest_weights, axis=1, keepdims=True
        )
        out_ref[here, :] = jnp.dot(
            weights.astype(jnp.bfloat16), values, preferred_element_type=jnp.float32
        ) + jnp.dot(
            newest_weights.astype(jnp.bfloat16), fresh_ref[1], preferred_element_type=jnp.float32
        )
        high_ref[here, :] = jnp.broadcast_to(high, (rows, HEAD_SIZE))
        sum_ref[here, :] = jnp.broadcast_to(total, (rows, HEAD_SIZE))


def prefix_nodes(first, index_ref, count_ref, length_ref, cache_ref, heads_ref, acc, high, total):
    nodes, _, length, _ = cache_ref.shape
    columns = lax.broadcasted_iota(jnp.int32, (1, length), 1)

    def one_node(node, carry):
        place = first + node
        valid = columns < length_ref[place]

        def one_tile(tile, inner):
            where = [
                pl.multiple_of(index_ref[place, tile * TILE + slot] * GROUP, GROUP)
                for slot in range(TILE)
            ]
            query = jnp.concatenate(
                [heads_ref[pl.ds(at, GROUP), :] for at in where], axis=0
            ).astype(jnp.bfloat16)
            scores = jnp.where(valid, nt(query, cache_ref[node, 0]) * SCALE, LOW)
            part_high = jnp.max(scores, axis=1, keepdims=True)
            weights = jnp.exp(scores - part_high)
            part_sum = jnp.sum(weights, axis=1, keepdims=True)
            part_out = jnp.dot(
                weights.astype(jnp.bfloat16), cache_ref[node, 1], preferred_element_type=jnp.float32
            )
            old_high = jnp.concatenate([high[pl.ds(at, GROUP), :] for at in where], axis=0)
            old_sum = jnp.concatenate([total[pl.ds(at, GROUP), :] for at in where], axis=0)
            old_out = jnp.concatenate([acc[pl.ds(at, GROUP), :] for at in where], axis=0)
            new_high = jnp.maximum(old_high, part_high)
            old_factor = jnp.exp(old_high - new_high)
            part_factor = jnp.exp(part_high - new_high)
            new_sum = old_sum * old_factor + part_sum * part_factor
            new_out = old_out * old_factor + part_out * part_factor
            for slot, at in enumerate(where):
                rows = slice(slot * GROUP, (slot + 1) * GROUP)
                high[pl.ds(at, GROUP), :] = new_high[rows]
                total[pl.ds(at, GROUP), :] = new_sum[rows]
                acc[pl.ds(at, GROUP), :] = new_out[rows]
            return inner

        lax.fori_loop(0, (count_ref[place] + TILE - 1) // TILE, one_tile, 0)
        return carry

    lax.fori_loop(0, nodes, one_node, 0)


def prefix_kernel(
    index_ref, count_ref, length_ref, group_ref,
    query_ref, cache_a, cache_b, cache_c, cache_d, own_out, own_high, own_sum,
    sent_ref, heads_ref, acc, high, total,
):
    requests = query_ref.shape[0]
    spread_heads(query_ref, heads_ref)
    heads_ref[requests * GROUP :, :] = jnp.zeros((GROUP, HEAD_SIZE), jnp.float32)
    acc[...] = jnp.zeros(acc.shape, jnp.float32)
    total[...] = jnp.zeros(total.shape, jnp.float32)
    high[...] = jnp.full(high.shape, LOW, jnp.float32)
    own_rows = own_out.shape[0]
    own = pl.ds(pl.multiple_of(group_ref[0] * own_rows, own_rows), own_rows)
    acc[own, :] = own_out[...]
    high[own, :] = own_high[...]
    total[own, :] = own_sum[...]
    first = 0
    for cache_ref in (cache_a, cache_b, cache_c, cache_d):
        prefix_nodes(first, index_ref, count_ref, length_ref, cache_ref, heads_ref, acc, high, total)
        first += cache_ref.shape[0]
    lanes = lax.broadcasted_iota(jnp.int32, (1, 128), 1)
    stats = jnp.zeros((requests, 128), jnp.float32)
    for head in range(GROUP):
        rows = pl.ds(head, requests, stride=GROUP)
        sent_ref[:, head * HEAD_SIZE : (head + 1) * HEAD_SIZE] = acc[rows, :]
        stats = jnp.where(lanes == head, high[rows, :], stats)
        stats = jnp.where(lanes == GROUP + head, total[rows, :], stats)
    sent_ref[:, WIDTH:] = stats


def final_kernel(parts_ref, out_ref):
    sources, heads_kv = parts_ref.shape[:2]
    for group in range(heads_kv):
        stats = [parts_ref[source, group, :, WIDTH:] for source in range(sources)]
        best = stats[0]
        for stat in stats[1:]:
            best = jnp.maximum(best, stat)
        factors = [jnp.exp(jnp.minimum(stat - best, 0.0)) for stat in stats]
        for head in range(GROUP):
            columns = slice(head * HEAD_SIZE, (head + 1) * HEAD_SIZE)
            numer = 0.0
            denom = 0.0
            for source in range(sources):
                factor = factors[source][:, head : head + 1]
                numer = numer + factor * parts_ref[source, group, :, columns]
                denom = denom + factor * stats[source][:, GROUP + head : GROUP + head + 1]
            start = group * WIDTH + head * HEAD_SIZE
            out_ref[:, start : start + HEAD_SIZE] = (numer / denom).astype(jnp.bfloat16)


def shards(
    queries, paths, node_owner, node_len, suf_len, prefix_kv, suffix_key_value, fresh_key_value
):
    x, zh, zl, core, kv = [lax.axis_index(name) for name in AXES]
    xs, zhs, zls, cores, kvs = [lax.axis_size(name) for name in AXES]
    rows_each = queries.shape[0]
    request_count = paths.shape[0]
    node_ids = lax.iota(jnp.int32, node_owner.shape[0])
    with jax.named_scope("send_queries"):
        my_paths = lax.dynamic_slice_in_dim(paths, kv * rows_each, rows_each, 0)
        my_holders = jnp.sum(
            jnp.where(my_paths[:, :, None] == node_ids, node_owner, 0), axis=-1
        )
        tail = jnp.pad(my_holders, ((0, 0), (0, 128 - PATH))).astype(jnp.bfloat16)
        by_head = queries.reshape(rows_each, kvs, WIDTH).transpose(1, 0, 2)
        outgoing = jnp.concatenate(
            [by_head, jnp.broadcast_to(tail[None], (kvs, rows_each, 128))], axis=-1
        )
        outgoing = jnp.broadcast_to(outgoing[None], (zhs,) + outgoing.shape)
        received = lax.all_to_all(
            outgoing.reshape(zhs * kvs, rows_each, PAD_WIDTH),
            ("zh", "kv"), split_axis=0, concat_axis=0, tiled=True,
        ).reshape(zhs * request_count, PAD_WIDTH)
    with jax.named_scope("send_prefix"):
        own_cache = prefix_kv[0]
        swap = [(0, 1), (1, 0)]

        def over_x(block):
            return lax.all_to_all(
                jnp.broadcast_to(block[None], (xs,) + block.shape), "x",
                split_axis=0, concat_axis=0, tiled=True,
            )

        cache_a = over_x(own_cache)
        other_cache = lax.ppermute(own_cache, "zl", swap)
        cache_c = over_x(other_cache)
        cache_b = lax.ppermute(cache_a, "core", swap)
        cache_d = lax.ppermute(cache_c, "core", swap)
    with jax.named_scope("suffix"):
        own_queries = lax.dynamic_slice_in_dim(received, zh * request_count, request_count, 0)
        length = suffix_key_value.shape[2]
        valid = (lax.iota(jnp.int32, length)[None, :] < suf_len[:, None]).astype(jnp.int32)
        local = jax.ShapeDtypeStruct((request_count * GROUP, HEAD_SIZE), jnp.float32)
        own_out, own_high, own_sum = pl.pallas_call(
            suffix_kernel,
            out_shape=(local, local, local),
            scratch_shapes=[pltpu.VMEM((request_count * GROUP, HEAD_SIZE), jnp.float32)],
            compiler_params=pltpu.CompilerParams(vmem_limit_bytes=32 * 1024 * 1024),
            name="suffix_attention",
        )(
            own_queries,
            suffix_key_value,
            fresh_key_value.transpose(1, 0, 2),
            valid.reshape(-1, 8 * length),
        )
    with jax.named_scope("prefix"):
        requests = zhs * request_count
        named = received[:, WIDTH : WIDTH + PATH].astype(jnp.int32)
        base = lax.iota(jnp.int32, xs) * (zhs * zls * cores) + zh * (zls * cores)
        held = jnp.concatenate(
            [
                base + side * cores + lane
                for side in (zl, zls - 1 - zl)
                for lane in (core, cores - 1 - core)
            ]
        )
        lengths = jnp.sum(jnp.where(held[:, None] == node_ids, node_len, 0), axis=-1)
        member = jnp.any(named[None] == held[:, None, None], axis=-1)
        rank = jnp.cumsum(member.astype(jnp.int32), axis=1) - 1
        counts = jnp.sum(member.astype(jnp.int32), axis=1)
        slot_ids = lax.iota(jnp.int32, SLOTS)
        hit = member[:, None, :] & (rank[:, None, :] == slot_ids[None, :, None])
        request_ids = lax.iota(jnp.int32, requests)
        index = jnp.sum(jnp.where(hit, request_ids, 0), axis=-1)
        index = jnp.where(slot_ids[None, :] < counts[:, None], index, requests)
        smem = pl.BlockSpec(memory_space=pltpu.SMEM)
        vmem = pl.BlockSpec(memory_space=pltpu.VMEM)
        scratch = pltpu.VMEM(((requests + 1) * GROUP, HEAD_SIZE), jnp.float32)
        sent = pl.pallas_call(
            prefix_kernel,
            out_shape=jax.ShapeDtypeStruct((requests, PAD_WIDTH), jnp.float32),
            in_specs=[smem] * 4 + [vmem] * 8,
            out_specs=vmem,
            scratch_shapes=[scratch] * 4,
            compiler_params=pltpu.CompilerParams(vmem_limit_bytes=40 * 1024 * 1024),
            name="prefix_attention",
        )(
            index, counts, lengths, zh[None],
            received, cache_a, cache_b, cache_c, cache_d, own_out, own_high, own_sum,
        )
    with jax.named_scope("send_parts"):
        parts = lax.all_to_all(
            sent.reshape(zhs * kvs, rows_each, PAD_WIDTH),
            ("zh", "kv"), split_axis=0, concat_axis=0, tiled=True,
        ).reshape(zhs, kvs, rows_each, PAD_WIDTH)
    with jax.named_scope("combine"):
        return pl.pallas_call(
            final_kernel,
            out_shape=jax.ShapeDtypeStruct((rows_each, kvs * WIDTH), jnp.bfloat16),
            compiler_params=pltpu.CompilerParams(vmem_limit_bytes=32 * 1024 * 1024),
            name="combine_parts",
        )(parts)


def solution(mesh):
    owners, kvs = mesh.devices.shape
    split = Mesh(mesh.devices.reshape(4, 4, 2, 2, kvs), AXES)
    return jax.shard_map(
        shards,
        mesh=split,
        in_specs=(
            P(AXES, None),
            P(OWNER, None),
            P(),
            P(),
            P(OWNER),
            P(OWNER, None, None, "kv"),
            P(OWNER, None, None, "kv"),
            P(OWNER, None, "kv"),
        ),
        out_specs=P(AXES, None),
        check_vma=False,
    )
```

time: 220 us -> 117 us (0.53)
  the two profiles are of different devices: /device:TPU:16 before, /device:TPU:8 now
where the time goes in v1:
time: 117 us; the launch traced here: 116 us
  blocking collectives  62.4 us (53%)
  waiting for transfers between devices  17.7 us (15%)
  starting transfers between devices  15 us (13%)
  Pallas kernels  11.2 us (10%)
  local copies, waits for them, and re-layouts  8.45 us (7%)
  other arithmetic  1.44 us (1%)
    all_to_all x1, blocking collectives, shards(): lax.all_to_all(outgoing.reshape(zhs * kvs, rows_each, PAD_WIDTH), ('zh',...  31.5 us
    all_to_all x1, blocking collectives, shards(): lax.all_to_all(sent.reshape(zhs * kvs, rows_each, PAD_WIDTH), ('zh', 'kv'...  30.9 us
    all_to_all x2, waiting for transfers between devices, over_x(): lax.all_to_all(jnp.broadcast_to(block[None], (xs,) + block.shape), 'x', s...  12.8 us
    pallas_call x1, Pallas kernels, shards(): pl.pallas_call(prefix_kernel, out_shape=jax.ShapeDtypeStruct((requests, P...  8.39 us
    all_to_all x2, starting transfers between devices, over_x(): lax.all_to_all(jnp.broadcast_to(block[None], (xs,) + block.shape), 'x', s...  7.81 us
    unnamed x17, local copies, waits for them, and re-layouts  5.34 us
    ppermute x1, waiting for transfers between devices, shards(): other_cache = lax.ppermute(own_cache, 'zl', swap)  4.92 us
    ppermute x1, starting transfers between devices, shards(): other_cache = lax.ppermute(own_cache, 'zl', swap)  3.33 us
  transfers between devices with their start and end apart: 5, of which 3 were waited for; matrix products, arithmetic and copies ran while one was open for 1% of the time, Pallas kernels for 1%

profile of v1, /device:TPU:8, one launch (start us, length us, event | category | flops | bytes accessed | tf_op | source)
XLA Modules:
  0.0 116.4 jit_solution(3656677508303082001)
XLA Ops:
  0.0 0.7 copy-done
  0.8 0.6 copy-done.4
  1.7 0.9 copy.24
  2.7 31.5 %all_to_all.20 = bf16[32,4,1152]{2,1,0:T(4,128)(2,1)S(1)} all-to-all(bf16[32,4,1152]{2,1,0:T(4,128)(2,1)S(1)} %bitcast.16), channel_id=1, replica_groups=mesh['x'=4,'zh'=4,'zl'=2,'core'=2,'kv'=8] {'zh','kv'}, dimensions={0} | all-to-all | bytes 589824 | tf_op jit(solution)/shard_map/send_queries/all_to_all | solution.py:184
  34.3 1.1 broadcast_in_dim.80
  35.4 4.3 %all-to-all-start.1 = ((bf16[4,2,512,128]{3,2,1,0:T(8,128)(2,1)}), bf16[4,2,512,128]{3,2,1,0:T(8,128)(2,1)S(1)}, u32[]{:S(2)}, u32[]{:S(2)}) async-start(bf16[4,2,512,128]{3,2,1,0:T(8,128)(2,1)} %broadcast_in_dim.80), calls=%async_computation.1 | async-start | bytes 2097152 | tf_op jit(solution)/shard_map/send_prefix/all_to_all | solution.py:193
  39.7 3.3 %collective-permute-start.1 = (bf16[2,512,128]{2,1,0:T(8,128)(2,1)S(1)}, bf16[2,512,128]{2,1,0:T(8,128)(2,1)S(1)}, u32[]{:S(2)}, u32[]{:S(2)}) collective-permute-start(bf16[2,512,128]{2,1,0:T(8,128)(2,1)S(1)} %bitcast.18), channel_id=1, source_target_pairs={{0,16},{16,0},{1,17},{17,1},{2,18},{18,2},{3,19},{19,3},{4,20},{20... | collective-permute-start | bytes 786440 | tf_op jit(solution)/shard_map/send_prefix/ppermute | solution.py:199
  43.0 4.9 %collective-permute-done.1 = bf16[2,512,128]{2,1,0:T(8,128)(2,1)S(1)} collective-permute-done((bf16[2,512,128]{2,1,0:T(8,128)(2,1)S(1)}, bf16[2,512,128]{2,1,0:T(8,128)(2,1)S(1)}, u32[]{:S(2)}, u32[]{:S(2)}) %collective-permute-start.1) | collective-permute-done | bytes 262176 | tf_op jit(solution)/shard_map/send_prefix/ppermute | solution.py:199
  47.9 5.2 %all-to-all-done.1.cache_a = bf16[4,2,512,128]{3,2,1,0:T(8,128)(2,1)S(1)} async-done(((bf16[4,2,512,128]{3,2,1,0:T(8,128)(2,1)}), bf16[4,2,512,128]{3,2,1,0:T(8,128)(2,1)S(1)}, u32[]{:S(2)}, u32[]{:S(2)}) %all-to-all-start.1) | async-done | bytes 1048608 | tf_op jit(solution)/shard_map/send_prefix/all_to_all | solution.py:193
  53.1 1.2 %broadcast_in_dim.81 = bf16[4,2,512,128]{3,2,1,0:T(8,128)(2,1)} broadcast(bf16[2,512,128]{2,1,0:T(8,128)(2,1)S(1)} %collective-permute-done.1), dimensions={1,2,3} | broadcast | bytes 1310720 | tf_op jit(solution)/shard_map/send_prefix/broadcast_in_dim | solution.py:194
  54.2 3.5 %all-to-all-start.2 = ((bf16[4,2,512,128]{3,2,1,0:T(8,128)(2,1)}), bf16[4,2,512,128]{3,2,1,0:T(8,128)(2,1)S(1)}, u32[]{:S(2)}, u32[]{:S(2)}) async-start(bf16[4,2,512,128]{3,2,1,0:T(8,128)(2,1)} %broadcast_in_dim.81), calls=%async_computation.2 | async-start | bytes 2097152 | tf_op jit(solution)/shard_map/send_prefix/all_to_all | solution.py:193
  57.8 0.6 copy-done.5
  58.8 0.6 copy-done.3
  59.5 0.6 copy-done.6
  60.4 1.9 %collective-permute-start = (bf16[4,2,512,128]{3,2,1,0:T(8,128)(2,1)S(1)}, bf16[4,2,512,128]{3,2,1,0:T(8,128)(2,1)}, u32[]{:S(2)}, u32[]{:S(2)}) collective-permute-start(bf16[4,2,512,128]{3,2,1,0:T(8,128)(2,1)S(1)} %all-to-all-done.1.cache_a), channel_id=1, source_target_pairs={{0,8},{8,0},{1,9},{9,1},{2,10},{10,2},{3,11},{11,3},{4,12},{12,4},... | collective-permute-start | bytes 3145736 | tf_op jit(solution)/shard_map/send_prefix/ppermute | solution.py:201
  62.3 7.7 %all-to-all-done.2.cache_c = bf16[4,2,512,128]{3,2,1,0:T(8,128)(2,1)S(1)} async-done(((bf16[4,2,512,128]{3,2,1,0:T(8,128)(2,1)}), bf16[4,2,512,128]{3,2,1,0:T(8,128)(2,1)S(1)}, u32[]{:S(2)}, u32[]{:S(2)}) %all-to-all-start.2) | async-done | bytes 1048608 | tf_op jit(solution)/shard_map/send_prefix/all_to_all | solution.py:193
  69.9 1.9 %collective-permute-start.2 = (bf16[4,2,512,128]{3,2,1,0:T(8,128)(2,1)S(1)}, bf16[4,2,512,128]{3,2,1,0:T(8,128)(2,1)}, u32[]{:S(2)}, u32[]{:S(2)}) collective-permute-start(bf16[4,2,512,128]{3,2,1,0:T(8,128)(2,1)S(1)} %all-to-all-done.2.cache_c), channel_id=1, source_target_pairs={{0,8},{8,0},{1,9},{9,1},{2,10},{10,2},{3,11},{11,3},{4,12},{12,4},... | collective-permute-start | bytes 3145736 | tf_op jit(solution)/shard_map/send_prefix/ppermute | solution.py:202
  72.0 0.3 reduce_window_sum.11
  72.3 1.2 %copy-done.1 = bf16[32,2,64,128]{3,2,1,0:T(8,128)(2,1)S(1)} copy-done((bf16[32,2,64,128]{3,2,1,0:T(8,128)(2,1)S(1)}, bf16[32,2,64,128]{3,2,1,0:T(8,128)(2,1)}, u32[]{:S(2)}) %copy-start.1) | copy-done | bytes 1048600
  73.6 1.2 %suffix_attention.1 = (f32[256,128]{1,0:T(8,128)S(1)}, f32[256,128]{1,0:T(8,128)S(1)}, f32[256,128]{1,0:T(8,128)S(1)}) custom-call(bf16[32,1152]{1,0:T(8,128)(2,1)S(1)} %constant_dynamic-slice_fusion.query_ref, bf16[32,2,64,128]{3,2,1,0:T(8,128)(2,1)S(1)} %copy-done.1, bf16[2,32,128]{2,1,0:T(8,128)(2,1)S(1)} %bitcast.15, ...), custom_call_target="tpu_custom_call" | custom-call | tf_op jit(solution)/shard_map/suffix/suffix_attention/pallas_call | solution.py:208
  74.9 0.4 select_reduce_fusion
  75.4 8.4 %prefix_attention.1 = f32[128,1152]{1,0:T(8,128)S(1)} custom-call(s32[16,32]{1,0:T(8,128)S(1)} %fusion.1.index_ref, s32[16]{0:T(128)S(1)} %convert_reduce_fusion.count_ref, s32[16]{0:T(128)S(1)} %select_reduce_fusion.1.length_ref, s32[1]{0:T(128)} %bitcast.2.group_ref, bf16[128,1152]{1,0:T(8,128)(2,1)S(1)} %reshape.41.query_ref, ...), custom_call_target="tpu_custom_call" | custom-call | tf_op jit(solution)/shard_map/prefix/prefix_attention/pallas_call | solution.py:243
  83.9 30.9 %all_to_all.21 = f32[32,4,1152]{2,1,0:T(4,128)S(1)} all-to-all(f32[32,4,1152]{2,1,0:T(4,128)S(1)} %reshape.42), channel_id=1, replica_groups=mesh['x'=4,'zh'=4,'zl'=2,'core'=2,'kv'=8] {'zh','kv'}, dimensions={0} | all-to-all | bytes 1179648 | tf_op jit(solution)/shard_map/send_parts/all_to_all | solution.py:256
  114.8 1.6 %combine_parts.1 = bf16[4,8192]{1,0:T(4,128)(2,1)} custom-call(f32[4,8,4,1152]{3,2,1,0:T(4,128)S(1)} %bitcast.14), custom_call_target="tpu_custom_call" | custom-call | tf_op jit(solution)/shard_map/combine/combine_parts/pallas_call | solution.py:261
  (40 shorter events, 1.7 us)
Async XLA Ops:
  0.0 0.7 copy-start
  0.7 0.7 copy-start.4
  2.7 31.5 %copy-start.2 = (bf16[1,2,512,128]{3,2,1,0:T(8,128)(2,1)S(1)}, bf16[1,2,512,128]{3,2,1,0:T(8,128)(2,1)}, u32[]{:S(2)}) copy-start(bf16[1,2,512,128]{3,2,1,0:T(8,128)(2,1)} %param.13) | copy-start | bytes 786436
  35.4 17.7 %all-to-all-start.1 = ((bf16[4,2,512,128]{3,2,1,0:T(8,128)(2,1)}), bf16[4,2,512,128]{3,2,1,0:T(8,128)(2,1)S(1)}, u32[]{:S(2)}, u32[]{:S(2)}) async-start(bf16[4,2,512,128]{3,2,1,0:T(8,128)(2,1)} %broadcast_in_dim.80), calls=%async_computation.1 | async-start | bytes 2097152 | tf_op jit(solution)/shard_map/send_prefix/all_to_all | solution.py:193
  39.7 8.3 %collective-permute-start.1 = (bf16[2,512,128]{2,1,0:T(8,128)(2,1)S(1)}, bf16[2,512,128]{2,1,0:T(8,128)(2,1)S(1)}, u32[]{:S(2)}, u32[]{:S(2)}) collective-permute-start(bf16[2,512,128]{2,1,0:T(8,128)(2,1)S(1)} %bitcast.18), channel_id=1, source_target_pairs={{0,16},{16,0},{1,17},{17,1},{2,18},{18,2},{3,19},{19,3},{4,20},{20... | collective-permute-start | bytes 786440 | tf_op jit(solution)/shard_map/send_prefix/ppermute | solution.py:199
  54.2 15.7 %all-to-all-start.2 = ((bf16[4,2,512,128]{3,2,1,0:T(8,128)(2,1)}), bf16[4,2,512,128]{3,2,1,0:T(8,128)(2,1)S(1)}, u32[]{:S(2)}, u32[]{:S(2)}) async-start(bf16[4,2,512,128]{3,2,1,0:T(8,128)(2,1)} %broadcast_in_dim.81), calls=%async_computation.2 | async-start | bytes 2097152 | tf_op jit(solution)/shard_map/send_prefix/all_to_all | solution.py:193
  57.8 0.7 copy-start.5
  58.7 0.7 copy-start.3
  59.4 0.7 copy-start.6
  60.4 15.0 %collective-permute-start = (bf16[4,2,512,128]{3,2,1,0:T(8,128)(2,1)S(1)}, bf16[4,2,512,128]{3,2,1,0:T(8,128)(2,1)}, u32[]{:S(2)}, u32[]{:S(2)}) collective-permute-start(bf16[4,2,512,128]{3,2,1,0:T(8,128)(2,1)S(1)} %all-to-all-done.1.cache_a), channel_id=1, source_target_pairs={{0,8},{8,0},{1,9},{9,1},{2,10},{10,2},{3,11},{11,3},{4,12},{12,4},... | collective-permute-start | bytes 3145736 | tf_op jit(solution)/shard_map/send_prefix/ppermute | solution.py:201
  69.9 5.4 %collective-permute-start.2 = (bf16[4,2,512,128]{3,2,1,0:T(8,128)(2,1)S(1)}, bf16[4,2,512,128]{3,2,1,0:T(8,128)(2,1)}, u32[]{:S(2)}, u32[]{:S(2)}) collective-permute-start(bf16[4,2,512,128]{3,2,1,0:T(8,128)(2,1)S(1)} %all-to-all-done.2.cache_c), channel_id=1, source_target_pairs={{0,8},{8,0},{1,9},{9,1},{2,10},{10,2},{3,11},{11,3},{4,12},{12,4},... | collective-permute-start | bytes 3145736 | tf_op jit(solution)/shard_map/send_prefix/ppermute | solution.py:202
  72.3 1.2 %copy-start.1 = (bf16[32,2,64,128]{3,2,1,0:T(8,128)(2,1)S(1)}, bf16[32,2,64,128]{3,2,1,0:T(8,128)(2,1)}, u32[]{:S(2)}) copy-start(bf16[32,2,64,128]{3,2,1,0:T(8,128)(2,1)} %cache_ref.1) | copy-start | bytes 3145732

commit v2 on v1

v2 whole, which is shorter than its diff:
```python
import jax
import jax.numpy as jnp
from jax import lax
from jax.experimental import pallas as pl
from jax.experimental.pallas import tpu as pltpu
from jax.sharding import Mesh
from jax.sharding import PartitionSpec as P

QUERY_HEADS = 64
KEY_VALUE_HEADS = 8
HEAD_SIZE = 128
PATH = 3
GROUP = QUERY_HEADS // KEY_VALUE_HEADS
WIDTH = GROUP * HEAD_SIZE
PAD_WIDTH = WIDTH + 128
SCALE = HEAD_SIZE ** (-0.5)
LOW = -1e30
EMPTY = -(2.0**20)
TILE = 16
LANES = 128
SPREAD = 80.0
AXES = ("x", "z", "core", "kv")
OWNER = ("x", "z", "core")


def nt(a, b):
    return lax.dot_general(a, b, (((1,), (1,)), ((), ())), preferred_element_type=jnp.float32)


def nn(a, b):
    return jnp.dot(a, b, preferred_element_type=jnp.float32)


def nearest(values, unit):
    return jnp.floor(values * (1.0 / unit) + 0.5) * unit


def make_plan(held_ref, named, plan_ref):
    requests = named.shape[0]
    nodes = held_ref.shape[0]
    lanes = lax.broadcasted_iota(jnp.int32, (1, LANES), 1)
    held = jnp.full((1, LANES), -1.0, jnp.float32)
    for node in range(nodes):
        held = jnp.where(lanes == node, held_ref[node].astype(jnp.float32), held)
    member = named[:, 0:1] == held
    for step in range(1, PATH):
        member = member | (named[:, step : step + 1] == held)
    member = member.astype(jnp.float32)
    row = lax.broadcasted_iota(jnp.int32, (requests, requests), 0)
    column = lax.broadcasted_iota(jnp.int32, (requests, requests), 1)
    earlier = (column < row).astype(jnp.float32).astype(jnp.bfloat16)
    rank = nn(earlier, member.astype(jnp.bfloat16))
    rank = jnp.where(member > 0, rank, -1.0)
    counts = jnp.sum(member, axis=0, keepdims=True)
    request_ids = lax.broadcasted_iota(jnp.int32, (8, requests), 1)
    request_ids = request_ids.astype(jnp.float32).astype(jnp.bfloat16)
    slots = lanes.astype(jnp.float32)
    for node in range(nodes):
        hit = (rank[:, node : node + 1] == slots).astype(jnp.float32).astype(jnp.bfloat16)
        index = nn(request_ids, hit)[0:1]
        count = counts[:, node : node + 1]
        index = jnp.where(slots < count, index, float(requests))
        index = jnp.where(lanes == LANES - 1, count, index)
        plan_ref[node : node + 1, :] = index.astype(jnp.int32)


def suffix_part(base, cache_ref, fresh_ref, valid_ref, heads_ref, acc, high, total):
    requests, _, length, _ = cache_ref.shape
    block = 8
    rows = block * GROUP
    row_request = lax.broadcasted_iota(jnp.int32, (rows, 1), 0) // GROUP
    key_request = lax.broadcasted_iota(jnp.int32, (1, block * length), 1) // length
    fresh_request = lax.broadcasted_iota(jnp.int32, (1, requests), 1)
    own_key = row_request == key_request
    for group in range(requests // block):
        here = pl.ds(pl.multiple_of(base + group * rows, rows), rows)
        query = heads_ref[here, :].astype(jnp.bfloat16)
        keys = cache_ref[group * block : (group + 1) * block, 0].reshape(block * length, HEAD_SIZE)
        values = cache_ref[group * block : (group + 1) * block, 1].reshape(block * length, HEAD_SIZE)
        usable = own_key & (valid_ref[group : group + 1, :] > 0)
        scores = jnp.where(usable, nt(query, keys) * SCALE, LOW)
        newest = jnp.where(
            fresh_request == row_request + group * block, nt(query, fresh_ref[0]) * SCALE, LOW
        )
        top = jnp.maximum(
            jnp.max(scores, axis=1, keepdims=True), jnp.max(newest, axis=1, keepdims=True)
        )
        weights = jnp.exp(scores - top)
        newest_weights = jnp.exp(newest - top)
        part_sum = jnp.sum(weights, axis=1, keepdims=True) + jnp.sum(
            newest_weights, axis=1, keepdims=True
        )
        acc[here, :] = nn(weights.astype(jnp.bfloat16), values) + nn(
            newest_weights.astype(jnp.bfloat16), fresh_ref[1]
        )
        high[here, :] = jnp.broadcast_to(top, (rows, HEAD_SIZE))
        total[here, :] = jnp.broadcast_to(part_sum, (rows, HEAD_SIZE))


def prefix_part(first, plan_ref, length_ref, cache_ref, heads_ref, acc, high, total):
    nodes, _, longest, _ = cache_ref.shape

    def one_node(node, carry):
        place = first + node
        length = length_ref[place]
        tiles = (plan_ref[place, LANES - 1] + TILE - 1) // TILE

        def tile_of(tokens):
            valid = lax.broadcasted_iota(jnp.int32, (1, tokens), 1) < length

            def one_tile(tile, inner):
                where = [
                    pl.multiple_of(plan_ref[place, tile * TILE + slot] * GROUP, GROUP)
                    for slot in range(TILE)
                ]
                query = jnp.concatenate(
                    [heads_ref[pl.ds(at, GROUP), :] for at in where], axis=0
                ).astype(jnp.bfloat16)
                scores = jnp.where(valid, nt(query, cache_ref[node, 0, :tokens]) * SCALE, LOW)
                part_high = jnp.max(scores, axis=1, keepdims=True)
                weights = jnp.exp(scores - part_high)
                part_sum = jnp.sum(weights, axis=1, keepdims=True)
                part_out = nn(weights.astype(jnp.bfloat16), cache_ref[node, 1, :tokens])
                old_high = jnp.concatenate([high[pl.ds(at, GROUP), :] for at in where], axis=0)
                old_sum = jnp.concatenate([total[pl.ds(at, GROUP), :] for at in where], axis=0)
                old_out = jnp.concatenate([acc[pl.ds(at, GROUP), :] for at in where], axis=0)
                new_high = jnp.maximum(old_high, part_high)
                old_factor = jnp.exp(old_high - new_high)
                part_factor = jnp.exp(part_high - new_high)
                new_sum = old_sum * old_factor + part_sum * part_factor
                new_out = old_out * old_factor + part_out * part_factor
                for slot, at in enumerate(where):
                    rows = slice(slot * GROUP, (slot + 1) * GROUP)
                    high[pl.ds(at, GROUP), :] = new_high[rows]
                    total[pl.ds(at, GROUP), :] = new_sum[rows]
                    acc[pl.ds(at, GROUP), :] = new_out[rows]
                return inner

            return one_tile

        small, middle = longest // 4, longest // 2
        for low, tokens in ((0, small), (small, middle), (middle, longest)):

            @pl.when((length > low) & (length <= tokens))
            def _():
                lax.fori_loop(0, tiles, tile_of(tokens), 0)

        return carry

    lax.fori_loop(0, nodes, one_node, 0)


def write_parts(sent_ref, acc, high, total):
    requests = sent_ref.shape[0]
    lanes = lax.broadcasted_iota(jnp.int32, (1, LANES), 1)
    highs = jnp.zeros((requests, LANES), jnp.float32)
    sums = jnp.zeros((requests, LANES), jnp.float32)
    powers = jnp.zeros((requests, LANES), jnp.float32)
    for head in range(GROUP):
        rows = pl.ds(head, requests, stride=GROUP)
        part_sum = total[rows, :]
        mean = acc[rows, :] / jnp.where(part_sum > 0, part_sum, 1.0)
        largest = jnp.max(jnp.abs(mean), axis=1, keepdims=True)
        power = jnp.ceil(jnp.log2(jnp.maximum(largest, 1e-30)))
        coded = jnp.exp(mean * (jnp.exp2(-power) * SPREAD))
        sent_ref[:, head * HEAD_SIZE : (head + 1) * HEAD_SIZE] = coded.astype(jnp.bfloat16)
        highs = jnp.where(lanes == head, high[rows, :], highs)
        sums = jnp.where(lanes == head, part_sum, sums)
        powers = jnp.where(lanes == head, power, powers)
    filled = sums > 0
    coarse = jnp.where(filled, nearest(highs, 64.0), EMPTY)
    rest = jnp.where(filled, highs - coarse + jnp.log(jnp.where(filled, sums, 1.0)), 0.0)
    middle = nearest(rest, 0.25)
    fine = nearest(rest - middle, 2.0**-10)
    last = rest - middle - fine
    stats = jnp.where(lanes < GROUP, coarse, 0.0)
    for place, piece in enumerate((middle, fine, last, powers)):
        start = (place + 1) * GROUP
        moved = pltpu.roll(piece, start, 1)
        stats = jnp.where((lanes >= start) & (lanes < start + GROUP), moved, stats)
    sent_ref[:, WIDTH:] = stats.astype(jnp.bfloat16)


def attend_kernel(
    held_ref, length_ref, place_ref,
    query_ref, suffix_ref, fresh_ref, valid_ref, near_ref, far_ref,
    sent_ref,
    heads_ref, acc, high, total, plan_ref, plan_scalars, plan_sem,
):
    requests = query_ref.shape[0]
    make_plan(held_ref, query_ref[:, WIDTH:].astype(jnp.float32), plan_ref)
    plan_copy = pltpu.make_async_copy(plan_ref, plan_scalars, plan_sem)
    plan_copy.start()
    for head in range(GROUP):
        part = query_ref[:, head * HEAD_SIZE : (head + 1) * HEAD_SIZE].astype(jnp.float32)
        heads_ref[pl.ds(head, requests, stride=GROUP), :] = part
    heads_ref[requests * GROUP :, :] = jnp.zeros((GROUP, HEAD_SIZE), jnp.float32)
    acc[...] = jnp.zeros(acc.shape, jnp.float32)
    total[...] = jnp.zeros(total.shape, jnp.float32)
    high[...] = jnp.full(high.shape, LOW, jnp.float32)
    base = place_ref[0] * (suffix_ref.shape[0] * GROUP)
    suffix_part(base, suffix_ref, fresh_ref, valid_ref, heads_ref, acc, high, total)
    plan_copy.wait()
    first = 0
    for cache_ref in (near_ref, far_ref):
        prefix_part(first, plan_scalars, length_ref, cache_ref, heads_ref, acc, high, total)
        first += cache_ref.shape[0]
    write_parts(sent_ref, acc, high, total)


def combine_kernel(parts_ref, out_ref):
    sources, heads_kv, rows, _ = parts_ref.shape
    for group in range(heads_kv):
        pieces = []
        for source in range(0, sources, 2):
            stat = jnp.concatenate(
                [parts_ref[source + i, group, :, WIDTH:].astype(jnp.float32) for i in range(2)],
                axis=0,
            )
            pieces.append([stat[:, place * GROUP : (place + 1) * GROUP] for place in range(5)])
        best = pieces[0][0]
        for coarse, *_ in pieces[1:]:
            best = jnp.maximum(best, coarse)
        best = jnp.maximum(best[:rows], best[rows:])
        best = jnp.concatenate([best, best], axis=0)
        shares = [
            jnp.exp(coarse - best + (middle + fine + last))
            for coarse, middle, fine, last, _ in pieces
        ]
        denom = shares[0]
        for share in shares[1:]:
            denom = denom + share
        denom = denom[:rows] + denom[rows:]
        denom = jnp.concatenate([denom, denom], axis=0) * SPREAD
        factors = [
            share * jnp.exp2(power) / denom for share, (*_, power) in zip(shares, pieces)
        ]
        for head in range(GROUP):
            columns = slice(head * HEAD_SIZE, (head + 1) * HEAD_SIZE)
            result = 0.0
            for pair, factor in enumerate(factors):
                coded = jnp.concatenate(
                    [
                        parts_ref[2 * pair + i, group, :, columns].astype(jnp.float32)
                        for i in range(2)
                    ],
                    axis=0,
                )
                result = result + factor[:, head : head + 1] * jnp.log(coded)
            start = group * WIDTH + head * HEAD_SIZE
            out_ref[:, start : start + HEAD_SIZE] = (result[:rows] + result[rows:]).astype(
                jnp.bfloat16
            )


def shards(
    queries, paths, node_owner, node_len, suf_len, prefix_kv, suffix_key_value, fresh_key_value
):
    x, z, core, kv = [lax.axis_index(name) for name in AXES]
    xs, zs, cores, kvs = [lax.axis_size(name) for name in AXES]
    rows_each = queries.shape[0]
    request_count = paths.shape[0]
    requests = zs * request_count
    node_ids = lax.iota(jnp.int32, node_owner.shape[0])
    smem = pl.BlockSpec(memory_space=pltpu.SMEM)
    vmem = pl.BlockSpec(memory_space=pltpu.VMEM)

    def exchange(slabs):
        return lax.all_to_all(slabs, ("z", "kv"), split_axis=0, concat_axis=0, tiled=True)

    with jax.named_scope("send_queries"):
        my_paths = lax.dynamic_slice_in_dim(paths, kv * rows_each, rows_each, 0)
        my_holders = jnp.sum(
            jnp.where(my_paths[:, :, None] == node_ids, node_owner, 0), axis=-1
        )
        tail = jnp.pad(my_holders, ((0, 0), (0, LANES - PATH))).astype(jnp.bfloat16)
        by_head = queries.reshape(rows_each, kvs, WIDTH).transpose(1, 0, 2)
        outgoing = jnp.concatenate(
            [by_head, jnp.broadcast_to(tail[None], (kvs, rows_each, LANES))], axis=-1
        )
        outgoing = jnp.broadcast_to(outgoing[None], (zs,) + outgoing.shape)
        outgoing, own_cache = lax.optimization_barrier((outgoing, prefix_kv))
    with jax.named_scope("send_prefix"):
        ring = [own_cache]
        for step in range(1, xs):
            hops = [(i, (i + step) % xs) for i in range(xs)]
            ring.append(lax.ppermute(own_cache, "x", hops))
        near = jnp.concatenate(ring, axis=0)
        far = lax.ppermute(near, "core", [(0, 1), (1, 0)])
    with jax.named_scope("send_queries"):
        received = exchange(outgoing.reshape(zs * kvs, rows_each, PAD_WIDTH))
        received = received.reshape(requests, PAD_WIDTH)
    with jax.named_scope("attend"):
        chip = (x - lax.iota(jnp.int32, xs)) % xs
        held = jnp.concatenate([(chip * zs + z) * cores + lane for lane in (core, cores - 1 - core)])
        lengths = jnp.sum(jnp.where(held[:, None] == node_ids, node_len, 0), axis=-1)
        length = suffix_key_value.shape[2]
        valid = (lax.iota(jnp.int32, length)[None, :] < suf_len[:, None]).astype(jnp.int32)
        rows = pltpu.VMEM(((requests + 1) * GROUP, HEAD_SIZE), jnp.float32)
        plan = (xs * cores, LANES)
        sent = pl.pallas_call(
            attend_kernel,
            out_shape=jax.ShapeDtypeStruct((requests, PAD_WIDTH), jnp.bfloat16),
            in_specs=[smem] * 3 + [vmem] * 6,
            out_specs=vmem,
            scratch_shapes=[rows] * 4
            + [
                pltpu.VMEM(plan, jnp.int32),
                pltpu.SMEM(plan, jnp.int32),
                pltpu.SemaphoreType.DMA,
            ],
            compiler_params=pltpu.CompilerParams(vmem_limit_bytes=40 * 1024 * 1024),
            name="attend",
        )(
            held, lengths, z[None],
            received, suffix_key_value, fresh_key_value.transpose(1, 0, 2),
            valid.reshape(-1, 8 * length), near, far,
        )
    with jax.named_scope("send_parts"):
        parts = exchange(sent.reshape(zs * kvs, rows_each, PAD_WIDTH))
        parts = parts.reshape(zs, kvs, rows_each, PAD_WIDTH)
    with jax.named_scope("combine"):
        return pl.pallas_call(
            combine_kernel,
            out_shape=jax.ShapeDtypeStruct((rows_each, kvs * WIDTH), jnp.bfloat16),
            compiler_params=pltpu.CompilerParams(vmem_limit_bytes=32 * 1024 * 1024),
            name="combine",
        )(parts)


def solution(mesh):
    owners, kvs = mesh.devices.shape
    split = Mesh(mesh.devices.reshape(4, 8, 2, kvs), AXES)
    return jax.shard_map(
        shards,
        mesh=split,
        in_specs=(
            P(AXES, None),
            P(OWNER, None),
            P(),
            P(),
            P(OWNER),
            P(OWNER, None, None, "kv"),
            P(OWNER, None, None, "kv"),
            P(OWNER, None, "kv"),
        ),
        out_specs=P(AXES, None),
        check_vma=False,
    )
```

time: 117 us -> 88.8 us (0.76)
  blocking collectives: 62.4 us -> 25.7 us
  starting transfers between devices: 15 us -> 30 us
  local copies, waits for them, and re-layouts: 8.45 us -> 4.11 us
    all_to_all x2 -> x1, blocking collectives: 62.4 us -> 25.7 us  [exchange(): lax.all_to_all(slabs, ('z', 'kv'), split_axis=0, concat_axis=0, tiled=True)]
    all_to_all x2 -> x1, starting transfers between devices: 7.81 us -> 16.6 us  [exchange(): lax.all_to_all(slabs, ('z', 'kv'), split_axis=0, concat_axis=0, tiled=True)]
    ppermute x3 -> x4, starting transfers between devices: 7.16 us -> 13.4 us  [the longest x3 11.4 us: shards(): ring.append(lax.ppermute(own_cache, 'x', hops))]
    ppermute x3 -> x4, waiting for transfers between devices: 4.93 us -> 0.01 us  [the longest x3 0.01 us: shards(): ring.append(lax.ppermute(own_cache, 'x', hops))]
    all_to_all x2 -> x1, waiting for transfers between devices: 12.8 us -> 17 us  [exchange(): lax.all_to_all(slabs, ('z', 'kv'), split_axis=0, concat_axis=0, tiled=True)]
    unnamed x17 -> x20, local copies, waits for them, and re-layouts: 5.34 us -> 2.37 us
    broadcast_in_dim x4 -> x2, local copies, waits for them, and re-layouts: 2.38 us -> 1 us  [the longest x1 1 us: shards(): outgoing = jnp.broadcast_to(outgoing[None], (zs,) + outgoing.shape)]
    pallas_call x3 -> x2, Pallas kernels: 11.2 us -> 10.8 us  [the longest x1 8.36 us: shards(): pl.pallas_call(attend_kernel, out_shape=jax.ShapeDtypeStruct((requests, P...]
  transfers between devices with their start and end apart: 5 -> 5, of which waited for: 3 -> 1; matrix products, arithmetic and copies ran while one was open for 1% -> 1% of each run, Pallas kernels for 1% -> 0%
where the time goes in v2:
time: 88.8 us; the launch traced here: 88.4 us
  starting transfers between devices  30 us (34%)
  blocking collectives  25.7 us (29%)
  waiting for transfers between devices  17 us (19%)
  Pallas kernels  10.8 us (12%)
  local copies, waits for them, and re-layouts  4.11 us (5%)
    all_to_all x1, blocking collectives, exchange(): lax.all_to_all(slabs, ('z', 'kv'), split_axis=0, concat_axis=0, tiled=True)  25.7 us
    all_to_all x1, waiting for transfers between devices, exchange(): lax.all_to_all(slabs, ('z', 'kv'), split_axis=0, concat_axis=0, tiled=True)  17 us
    all_to_all x1, starting transfers between devices, exchange(): lax.all_to_all(slabs, ('z', 'kv'), split_axis=0, concat_axis=0, tiled=True)  16.6 us
    ppermute x3, starting transfers between devices, shards(): ring.append(lax.ppermute(own_cache, 'x', hops))  11.4 us
    pallas_call x1, Pallas kernels, shards(): pl.pallas_call(attend_kernel, out_shape=jax.ShapeDtypeStruct((requests, P...  8.36 us
    pallas_call x1, Pallas kernels, shards(): pl.pallas_call(combine_kernel, out_shape=jax.ShapeDtypeStruct((rows_each,...  2.4 us
    unnamed x20, local copies, waits for them, and re-layouts  2.37 us
    ppermute x1, starting transfers between devices, shards(): far = lax.ppermute(near, 'core', [(0, 1), (1, 0)])  2.05 us
  transfers between devices with their start and end apart: 5, of which 1 were waited for; matrix products, arithmetic and copies ran while one was open for 1% of the time, Pallas kernels for 0%

profile of v2, /device:TPU:8, one launch (start us, length us, event | category | flops | bytes accessed | tf_op | source)
XLA Modules:
  0.0 88.4 jit_solution(14729511963581296876)
XLA Ops:
  0.0 0.7 copy-done
  0.7 0.1 constant_dynamic-slice_fusion
  0.8 0.6 copy-done.4
  1.3 0.2 select_reduce_fusion
  1.6 0.1 copy.15
  1.7 0.9 copy.19
  2.6 1.0 %broadcast_in_dim.43 = bf16[8,8,4,1152]{3,2,1,0:T(4,128)(2,1)} broadcast(bf16[8,4,1152]{2,1,0:T(4,128)(2,1)S(1)} %copy.13), dimensions={1,2,3} | broadcast | bytes 663552 | tf_op jit(solution)/shard_map/send_queries/broadcast_in_dim | solution.py:281
  3.6 3.4 %collective-permute-start = (bf16[1,2,512,128]{3,2,1,0:T(8,128)(2,1)S(1)}, bf16[1,2,512,128]{3,2,1,0:T(8,128)(2,1)S(1)}, u32[]{:S(2)}, u32[]{:S(2)}) collective-permute-start(bf16[1,2,512,128]{3,2,1,0:T(8,128)(2,1)S(1)} %copy-done.2), channel_id=1, source_target_pairs={{0,128},{128,256},{256,384},{384,0},{1,129},{129,257},{257,385},{3... | collective-permute-start | bytes 786440 | tf_op jit(solution)/shard_map/send_prefix/ppermute | solution.py:287
  7.0 4.6 %collective-permute-start.1 = (bf16[1,2,512,128]{3,2,1,0:T(8,128)(2,1)S(1)}, bf16[1,2,512,128]{3,2,1,0:T(8,128)(2,1)S(1)}, u32[]{:S(2)}, u32[]{:S(2)}) collective-permute-start(bf16[1,2,512,128]{3,2,1,0:T(8,128)(2,1)S(1)} %copy-done.2), channel_id=1, source_target_pairs={{0,256},{128,384},{256,0},{384,128},{1,257},{129,385},{257,1},{385... | collective-permute-start | bytes 786440 | tf_op jit(solution)/shard_map/send_prefix/ppermute | solution.py:287
  11.7 3.3 %collective-permute-start.2 = (bf16[1,2,512,128]{3,2,1,0:T(8,128)(2,1)S(1)}, bf16[1,2,512,128]{3,2,1,0:T(8,128)(2,1)S(1)}, u32[]{:S(2)}, u32[]{:S(2)}) collective-permute-start(bf16[1,2,512,128]{3,2,1,0:T(8,128)(2,1)S(1)} %copy-done.2), channel_id=1, source_target_pairs={{0,384},{128,0},{256,128},{384,256},{1,385},{129,1},{257,129},{385... | collective-permute-start | bytes 786440 | tf_op jit(solution)/shard_map/send_prefix/ppermute | solution.py:287
  15.0 16.6 %all-to-all-start = ((bf16[64,4,1152]{2,1,0:T(4,128)(2,1)}), bf16[64,4,1152]{2,1,0:T(4,128)(2,1)S(1)}, u32[]{:S(2)}, u32[]{:S(2)}) async-start(bf16[64,4,1152]{2,1,0:T(4,128)(2,1)} %bitcast.2), calls=%async_computation | async-start | bytes 1179648 | tf_op jit(solution)/shard_map/send_queries/all_to_all | solution.py:269
  31.9 2.1 %collective-permute-start.3 = (bf16[4,2,512,128]{3,2,1,0:T(8,128)(2,1)S(1)}, bf16[4,2,512,128]{3,2,1,0:T(8,128)(2,1)}, u32[]{:S(2)}, u32[]{:S(2)}) collective-permute-start(bf16[4,2,512,128]{3,2,1,0:T(8,128)(2,1)S(1)} %constant_dynamic-update-slice_fusion.near_ref), channel_id=1, source_target_pairs={{0,8},{8,0},{1,9},{9,1},{2,10},{10,2},{3,11},{11,3},{4,12},{12,4},... | collective-permute-start | bytes 3145736 | tf_op jit(solution)/shard_map/send_prefix/ppermute | solution.py:289
  33.9 0.1 lt.36
  34.0 0.1 lt.37
  34.1 0.1 lt.38
  34.2 0.1 lt.34
  34.3 0.1 pad_add_fusion.held_ref
  34.4 0.2 select_reduce_fusion.1.length_ref
  34.6 17.0 %all-to-all-done = bf16[64,4,1152]{2,1,0:T(4,128)(2,1)S(1)} async-done(((bf16[64,4,1152]{2,1,0:T(4,128)(2,1)}), bf16[64,4,1152]{2,1,0:T(4,128)(2,1)S(1)}, u32[]{:S(2)}, u32[]{:S(2)}) %all-to-all-start) | async-done | bytes 589856 | tf_op jit(solution)/shard_map/send_queries/all_to_all | solution.py:269
  51.6 0.1 reshape.27.query_ref
  51.7 8.4 %attend.1 = bf16[256,1152]{1,0:T(8,128)(2,1)S(1)} custom-call(s32[8]{0:T(128)S(1)} %pad_add_fusion.held_ref, s32[8]{0:T(128)S(1)} %select_reduce_fusion.1.length_ref, s32[1]{0:T(128)} %bitcast.place_ref, bf16[256,1152]{1,0:T(8,128)(2,1)S(1)} %reshape.27.query_ref, bf16[32,2,64,128]{3,2,1,0:T(8,128)(2,1)S(1)} %copy-done.1, bf16[2,32,128]{2,1,0:T(8,128)(2,1)S(1)} %bitcast.14, ...), custom_call_target="tpu_custom_call" | custom-call | tf_op jit(solution)/shard_map/attend/attend/pallas_call | solution.py:301
  60.1 0.1 reshape.28
  60.3 25.7 %all_to_all.10 = bf16[64,4,1152]{2,1,0:T(4,128)(2,1)S(1)} all-to-all(bf16[64,4,1152]{2,1,0:T(4,128)(2,1)S(1)} %reshape.28), channel_id=1, replica_groups=mesh['x'=4,'z'=8,'core'=2,'kv'=8] {'z','kv'}, dimensions={0} | all-to-all | bytes 1179648 | tf_op jit(solution)/shard_map/send_parts/all_to_all | solution.py:269
  86.0 2.4 %combine.1 = bf16[4,8192]{1,0:T(4,128)(2,1)} custom-call(bf16[8,8,4,1152]{3,2,1,0:T(4,128)(2,1)S(1)} %bitcast.13), custom_call_target="tpu_custom_call" | custom-call | tf_op jit(solution)/shard_map/combine/combine/pallas_call | solution.py:323
  (29 shorter events, 0.3 us)
Async XLA Ops:
  0.0 0.7 copy-start
  0.7 0.7 copy-start.4
  2.6 1.0 %copy-start.2 = (bf16[1,2,512,128]{3,2,1,0:T(8,128)(2,1)S(1)}, bf16[1,2,512,128]{3,2,1,0:T(8,128)(2,1)}, u32[]{:S(2)}) copy-start(bf16[1,2,512,128]{3,2,1,0:T(8,128)(2,1)} %param.13) | copy-start | bytes 786436
  3.6 28.0 %collective-permute-start = (bf16[1,2,512,128]{3,2,1,0:T(8,128)(2,1)S(1)}, bf16[1,2,512,128]{3,2,1,0:T(8,128)(2,1)S(1)}, u32[]{:S(2)}, u32[]{:S(2)}) collective-permute-start(bf16[1,2,512,128]{3,2,1,0:T(8,128)(2,1)S(1)} %copy-done.2), channel_id=1, source_target_pairs={{0,128},{128,256},{256,384},{384,0},{1,129},{129,257},{257,385},{3... | collective-permute-start | bytes 786440 | tf_op jit(solution)/shard_map/send_prefix/ppermute | solution.py:287
  7.0 24.7 %collective-permute-start.1 = (bf16[1,2,512,128]{3,2,1,0:T(8,128)(2,1)S(1)}, bf16[1,2,512,128]{3,2,1,0:T(8,128)(2,1)S(1)}, u32[]{:S(2)}, u32[]{:S(2)}) collective-permute-start(bf16[1,2,512,128]{3,2,1,0:T(8,128)(2,1)S(1)} %copy-done.2), channel_id=1, source_target_pairs={{0,256},{128,384},{256,0},{384,128},{1,257},{129,385},{257,1},{385... | collective-permute-start | bytes 786440 | tf_op jit(solution)/shard_map/send_prefix/ppermute | solution.py:287
  11.7 20.1 %collective-permute-start.2 = (bf16[1,2,512,128]{3,2,1,0:T(8,128)(2,1)S(1)}, bf16[1,2,512,128]{3,2,1,0:T(8,128)(2,1)S(1)}, u32[]{:S(2)}, u32[]{:S(2)}) collective-permute-start(bf16[1,2,512,128]{3,2,1,0:T(8,128)(2,1)S(1)} %copy-done.2), channel_id=1, source_target_pairs={{0,384},{128,0},{256,128},{384,256},{1,385},{129,1},{257,129},{385... | collective-permute-start | bytes 786440 | tf_op jit(solution)/shard_map/send_prefix/ppermute | solution.py:287
  15.0 36.6 %all-to-all-start = ((bf16[64,4,1152]{2,1,0:T(4,128)(2,1)}), bf16[64,4,1152]{2,1,0:T(4,128)(2,1)S(1)}, u32[]{:S(2)}, u32[]{:S(2)}) async-start(bf16[64,4,1152]{2,1,0:T(4,128)(2,1)} %bitcast.2), calls=%async_computation | async-start | bytes 1179648 | tf_op jit(solution)/shard_map/send_queries/all_to_all | solution.py:269
  31.7 2.2 %copy-start.5 = (s32[32]{0:T(128)S(1)}, s32[32]{0:T(128)}, u32[]{:S(2)}) copy-start(s32[32]{0:T(128)} %param.12) | copy-start | bytes 388
  31.7 2.5 %copy-start.3 = (bf16[32,2,128]{2,1,0:T(2,128)(2,1)S(1)}, bf16[32,2,128]{2,1,0:T(2,128)(2,1)}, u32[]{:S(2)}) copy-start(bf16[32,2,128]{2,1,0:T(2,128)(2,1)} %param.15) | copy-start | bytes 49156
  31.7 2.6 %copy-start.6 = (s32[64]{0:T(128)S(1)}, s32[64]{0:T(128)}, u32[]{:S(2)}) copy-start(s32[64]{0:T(128)} %param.11) | copy-start | bytes 772
  31.8 19.9 %copy-start.1 = (bf16[32,2,64,128]{3,2,1,0:T(8,128)(2,1)S(1)}, bf16[32,2,64,128]{3,2,1,0:T(8,128)(2,1)}, u32[]{:S(2)}) copy-start(bf16[32,2,64,128]{3,2,1,0:T(8,128)(2,1)} %suffix_ref.1) | copy-start | bytes 3145732
  31.9 19.9 %collective-permute-start.3 = (bf16[4,2,512,128]{3,2,1,0:T(8,128)(2,1)S(1)}, bf16[4,2,512,128]{3,2,1,0:T(8,128)(2,1)}, u32[]{:S(2)}, u32[]{:S(2)}) collective-permute-start(bf16[4,2,512,128]{3,2,1,0:T(8,128)(2,1)S(1)} %constant_dynamic-update-slice_fusion.near_ref), channel_id=1, source_target_pairs={{0,8},{8,0},{1,9},{9,1},{2,10},{10,2},{3,11},{11,3},{4,12},{12,4},... | collective-permute-start | bytes 3145736 | tf_op jit(solution)/shard_map/send_prefix/ppermute | solution.py:289

commit v3 on v2

--- a/solution.py
+++ b/solution.py
@@ -21,6 +21,7 @@
 SPREAD = 80.0
 AXES = ("x", "z", "core", "kv")
 OWNER = ("x", "z", "core")
+SWAPS = (0, 1, 3, 2)
 
 
 def nt(a, b):
@@ -97,43 +98,53 @@
         total[here, :] = jnp.broadcast_to(part_sum, (rows, HEAD_SIZE))
 
 
-def prefix_part(first, plan_ref, length_ref, cache_ref, heads_ref, acc, high, total):
-    nodes, _, longest, _ = cache_ref.shape
-
-    def one_node(node, carry):
-        place = first + node
-        length = length_ref[place]
-        tiles = (plan_ref[place, LANES - 1] + TILE - 1) // TILE
+def prefix_part(plan_ref, length_ref, near_ref, far_ref, heads_ref, acc, high, total):
+    nodes, _, longest, _ = near_ref.shape
+
+    def one_pair(node, carry):
+        places = (node, node + nodes)
+        lengths = [length_ref[place] for place in places]
+        most = jnp.maximum(lengths[0], lengths[1])
+        count = jnp.maximum(plan_ref[places[0], LANES - 1], plan_ref[places[1], LANES - 1])
+        tiles = (count + TILE - 1) // TILE
 
         def tile_of(tokens):
-            valid = lax.broadcasted_iota(jnp.int32, (1, tokens), 1) < length
+            columns = lax.broadcasted_iota(jnp.int32, (1, tokens), 1)
+            masks = [columns < length for length in lengths]
 
             def one_tile(tile, inner):
                 where = [
-                    pl.multiple_of(plan_ref[place, tile * TILE + slot] * GROUP, GROUP)
-                    for slot in range(TILE)
+                    [
+                        pl.multiple_of(plan_ref[place, tile * TILE + slot] * GROUP, GROUP)
+                        for slot in range(TILE)
+                    ]
+                    for place in places
                 ]
-                query = jnp.concatenate(
-                    [heads_ref[pl.ds(at, GROUP), :] for at in where], axis=0
-                ).astype(jnp.bfloat16)
-                scores = jnp.where(valid, nt(query, cache_ref[node, 0, :tokens]) * SCALE, LOW)
-                part_high = jnp.max(scores, axis=1, keepdims=True)
-                weights = jnp.exp(scores - part_high)
-                part_sum = jnp.sum(weights, axis=1, keepdims=True)
-                part_out = nn(weights.astype(jnp.bfloat16), cache_ref[node, 1, :tokens])
-                old_high = jnp.concatenate([high[pl.ds(at, GROUP), :] for at in where], axis=0)
-                old_sum = jnp.concatenate([total[pl.ds(at, GROUP), :] for at in where], axis=0)
-                old_out = jnp.concatenate([acc[pl.ds(at, GROUP), :] for at in where], axis=0)
-                new_high = jnp.maximum(old_high, part_high)
-                old_factor = jnp.exp(old_high - new_high)
-                part_factor = jnp.exp(part_high - new_high)
-                new_sum = old_sum * old_factor + part_sum * part_factor
-                new_out = old_out * old_factor + part_out * part_factor
-                for slot, at in enumerate(where):
-                    rows = slice(slot * GROUP, (slot + 1) * GROUP)
-                    high[pl.ds(at, GROUP), :] = new_high[rows]
-                    total[pl.ds(at, GROUP), :] = new_sum[rows]
-                    acc[pl.ds(at, GROUP), :] = new_out[rows]
+                parts = []
+                for spots, mask, cache_ref in zip(where, masks, (near_ref, far_ref)):
+                    query = jnp.concatenate(
+                        [heads_ref[pl.ds(at, GROUP), :] for at in spots], axis=0
+                    ).astype(jnp.bfloat16)
+                    scores = jnp.where(mask, nt(query, cache_ref[node, 0, :tokens]) * SCALE, LOW)
+                    part_high = jnp.max(scores, axis=1, keepdims=True)
+                    weights = jnp.exp(scores - part_high)
+                    part_sum = jnp.sum(weights, axis=1, keepdims=True)
+                    part_out = nn(weights.astype(jnp.bfloat16), cache_ref[node, 1, :tokens])
+                    parts.append((part_high, part_sum, part_out))
+                for spots, (part_high, part_sum, part_out) in zip(where, parts):
+                    old_high = jnp.concatenate([high[pl.ds(at, GROUP), :] for at in spots], axis=0)
+                    old_sum = jnp.concatenate([total[pl.ds(at, GROUP), :] for at in spots], axis=0)
+                    old_out = jnp.concatenate([acc[pl.ds(at, GROUP), :] for at in spots], axis=0)
+                    new_high = jnp.maximum(old_high, part_high)
+                    old_factor = jnp.exp(old_high - new_high)
+                    part_factor = jnp.exp(part_high - new_high)
+                    new_sum = old_sum * old_factor + part_sum * part_factor
+                    new_out = old_out * old_factor + part_out * part_factor
+                    for slot, at in enumerate(spots):
+                        rows = slice(slot * GROUP, (slot + 1) * GROUP)
+                        high[pl.ds(at, GROUP), :] = new_high[rows]
+                        total[pl.ds(at, GROUP), :] = new_sum[rows]
+                        acc[pl.ds(at, GROUP), :] = new_out[rows]
                 return inner
 
             return one_tile
@@ -141,13 +152,13 @@
         small, middle = longest // 4, longest // 2
         for low, tokens in ((0, small), (small, middle), (middle, longest)):
 
-            @pl.when((length > low) & (length <= tokens))
+            @pl.when((most > low) & (most <= tokens))
             def _():
                 lax.fori_loop(0, tiles, tile_of(tokens), 0)
 
         return carry
 
-    lax.fori_loop(0, nodes, one_node, 0)
+    lax.fori_loop(0, nodes, one_pair, 0)
 
 
 def write_parts(sent_ref, acc, high, total):
@@ -155,18 +166,20 @@
     lanes = lax.broadcasted_iota(jnp.int32, (1, LANES), 1)
     highs = jnp.zeros((requests, LANES), jnp.float32)
     sums = jnp.zeros((requests, LANES), jnp.float32)
-    powers = jnp.zeros((requests, LANES), jnp.float32)
+    tops = jnp.zeros((requests, LANES), jnp.float32)
     for head in range(GROUP):
         rows = pl.ds(head, requests, stride=GROUP)
-        part_sum = total[rows, :]
-        mean = acc[rows, :] / jnp.where(part_sum > 0, part_sum, 1.0)
-        largest = jnp.max(jnp.abs(mean), axis=1, keepdims=True)
-        power = jnp.ceil(jnp.log2(jnp.maximum(largest, 1e-30)))
-        coded = jnp.exp(mean * (jnp.exp2(-power) * SPREAD))
+        top = jnp.max(jnp.abs(acc[rows, :]), axis=1, keepdims=True)
+        highs = jnp.where(lanes == head, high[rows, :], highs)
+        sums = jnp.where(lanes == head, total[rows, :], sums)
+        tops = jnp.where(lanes == head, top, tops)
+    share = 1.0 / jnp.where(sums > 0, sums, 1.0)
+    powers = jnp.ceil(jnp.log2(jnp.maximum(tops * share, 1e-30)))
+    factors = share * (jnp.exp2(-powers) * SPREAD)
+    for head in range(GROUP):
+        rows = pl.ds(head, requests, stride=GROUP)
+        coded = jnp.exp(acc[rows, :] * factors[:, head : head + 1])
         sent_ref[:, head * HEAD_SIZE : (head + 1) * HEAD_SIZE] = coded.astype(jnp.bfloat16)
-        highs = jnp.where(lanes == head, high[rows, :], highs)
-        sums = jnp.where(lanes == head, part_sum, sums)
-        powers = jnp.where(lanes == head, power, powers)
     filled = sums > 0
     coarse = jnp.where(filled, nearest(highs, 64.0), EMPTY)
     rest = jnp.where(filled, highs - coarse + jnp.log(jnp.where(filled, sums, 1.0)), 0.0)
@@ -181,30 +194,67 @@
     sent_ref[:, WIDTH:] = stats.astype(jnp.bfloat16)
 
 
-def attend_kernel(
-    held_ref, length_ref, place_ref,
-    query_ref, suffix_ref, fresh_ref, valid_ref, near_ref, far_ref,
-    sent_ref,
-    heads_ref, acc, high, total, plan_ref, plan_scalars, plan_sem,
+def pack_kernel(place_ref, paths_ref, owner_ref, query_ref, sent_ref):
+    heads_kv = KEY_VALUE_HEADS
+    copies = sent_ref.shape[0] // heads_kv
+    rows = query_ref.shape[0]
+    lanes = lax.broadcasted_iota(jnp.int32, (rows, LANES), 1)
+    sublanes = lax.broadcasted_iota(jnp.int32, (rows, LANES), 0)
+    tail = jnp.zeros((rows, LANES), jnp.float32)
+    for row in range(rows):
+        for step in range(PATH):
+            node = paths_ref[step, place_ref[0] * rows + row]
+            holder = owner_ref[node].astype(jnp.float32)
+            tail = jnp.where((sublanes == row) & (lanes == step), holder, tail)
+    tail = tail.astype(jnp.bfloat16)
+    for group in range(heads_kv):
+        part = query_ref[:, group * WIDTH : (group + 1) * WIDTH]
+        for copy in range(copies):
+            sent_ref[copy * heads_kv + group, :, :WIDTH] = part
+            sent_ref[copy * heads_kv + group, :, WIDTH:] = tail
+
+
+def local_kernel(
+    held_ref, query_ref, own_ref, fresh_ref, valid_ref, stored_ref,
+    plan_ref, heads_ref, acc, high, total,
+    own_heads_ref, suffix_ref, suffix_sem,
 ):
+    fetch = pltpu.make_async_copy(stored_ref, suffix_ref, suffix_sem)
+    fetch.start()
     requests = query_ref.shape[0]
     make_plan(held_ref, query_ref[:, WIDTH:].astype(jnp.float32), plan_ref)
-    plan_copy = pltpu.make_async_copy(plan_ref, plan_scalars, plan_sem)
-    plan_copy.start()
     for head in range(GROUP):
-        part = query_ref[:, head * HEAD_SIZE : (head + 1) * HEAD_SIZE].astype(jnp.float32)
+        columns = slice(head * HEAD_SIZE, (head + 1) * HEAD_SIZE)
+        part = query_ref[:, columns].astype(jnp.float32)
         heads_ref[pl.ds(head, requests, stride=GROUP), :] = part
+        part = own_ref[:, columns].astype(jnp.float32)
+        own_heads_ref[pl.ds(head, own_ref.shape[0], stride=GROUP), :] = part
     heads_ref[requests * GROUP :, :] = jnp.zeros((GROUP, HEAD_SIZE), jnp.float32)
+    fetch.wait()
+    suffix_part(0, suffix_ref, fresh_ref, valid_ref, own_heads_ref, acc, high, total)
+
+
+def prefix_kernel(
+    plan_ref, length_ref, place_ref,
+    heads_ref, own_out, own_high, own_sum, near_ref, far_ref,
+    sent_ref,
+    acc, high, total, near_cache, far_cache, near_sem, far_sem,
+):
+    near_fetch = pltpu.make_async_copy(near_ref, near_cache, near_sem)
+    far_fetch = pltpu.make_async_copy(far_ref, far_cache, far_sem)
+    near_fetch.start()
+    far_fetch.start()
     acc[...] = jnp.zeros(acc.shape, jnp.float32)
     total[...] = jnp.zeros(total.shape, jnp.float32)
     high[...] = jnp.full(high.shape, LOW, jnp.float32)
-    base = place_ref[0] * (suffix_ref.shape[0] * GROUP)
-    suffix_part(base, suffix_ref, fresh_ref, valid_ref, heads_ref, acc, high, total)
-    plan_copy.wait()
-    first = 0
-    for cache_ref in (near_ref, far_ref):
-        prefix_part(first, plan_scalars, length_ref, cache_ref, heads_ref, acc, high, total)
-        first += cache_ref.shape[0]
+    own_rows = own_out.shape[0]
+    own = pl.ds(pl.multiple_of(place_ref[0] * own_rows, own_rows), own_rows)
+    acc[own, :] = own_out[...]
+    high[own, :] = own_high[...]
+    total[own, :] = own_sum[...]
+    near_fetch.wait()
+    far_fetch.wait()
+    prefix_part(plan_ref, length_ref, near_cache, far_cache, heads_ref, acc, high, total)
     write_parts(sent_ref, acc, high, total)
 
 
@@ -261,61 +311,75 @@
     rows_each = queries.shape[0]
     request_count = paths.shape[0]
     requests = zs * request_count
-    node_ids = lax.iota(jnp.int32, node_owner.shape[0])
     smem = pl.BlockSpec(memory_space=pltpu.SMEM)
     vmem = pl.BlockSpec(memory_space=pltpu.VMEM)
+    anywhere = pl.BlockSpec(memory_space=pl.ANY)
+    hbm = pl.BlockSpec(memory_space=pltpu.HBM)
 
     def exchange(slabs):
         return lax.all_to_all(slabs, ("z", "kv"), split_axis=0, concat_axis=0, tiled=True)
 
     with jax.named_scope("send_queries"):
-        my_paths = lax.dynamic_slice_in_dim(paths, kv * rows_each, rows_each, 0)
-        my_holders = jnp.sum(
-            jnp.where(my_paths[:, :, None] == node_ids, node_owner, 0), axis=-1
-        )
-        tail = jnp.pad(my_holders, ((0, 0), (0, LANES - PATH))).astype(jnp.bfloat16)
-        by_head = queries.reshape(rows_each, kvs, WIDTH).transpose(1, 0, 2)
-        outgoing = jnp.concatenate(
-            [by_head, jnp.broadcast_to(tail[None], (kvs, rows_each, LANES))], axis=-1
-        )
-        outgoing = jnp.broadcast_to(outgoing[None], (zs,) + outgoing.shape)
+        outgoing = pl.pallas_call(
+            pack_kernel,
+            out_shape=jax.ShapeDtypeStruct((zs * kvs, rows_each, PAD_WIDTH), jnp.bfloat16),
+            in_specs=[smem] * 3 + [vmem],
+            out_specs=vmem,
+            name="pack_queries",
+        )(kv[None], paths.T, node_owner, queries)
         outgoing, own_cache = lax.optimization_barrier((outgoing, prefix_kv))
     with jax.named_scope("send_prefix"):
         ring = [own_cache]
-        for step in range(1, xs):
-            hops = [(i, (i + step) % xs) for i in range(xs)]
-            ring.append(lax.ppermute(own_cache, "x", hops))
+        for step in SWAPS[1:]:
+            ring.append(lax.ppermute(own_cache, "x", [(i, i ^ step) for i in range(xs)]))
         near = jnp.concatenate(ring, axis=0)
         far = lax.ppermute(near, "core", [(0, 1), (1, 0)])
     with jax.named_scope("send_queries"):
-        received = exchange(outgoing.reshape(zs * kvs, rows_each, PAD_WIDTH))
+        received = exchange(outgoing)
         received = received.reshape(requests, PAD_WIDTH)
     with jax.named_scope("attend"):
-        chip = (x - lax.iota(jnp.int32, xs)) % xs
+        node_ids = lax.iota(jnp.int32, node_len.shape[0])
+        chip = x ^ jnp.array(SWAPS, jnp.int32)
         held = jnp.concatenate([(chip * zs + z) * cores + lane for lane in (core, cores - 1 - core)])
         lengths = jnp.sum(jnp.where(held[:, None] == node_ids, node_len, 0), axis=-1)
         length = suffix_key_value.shape[2]
         valid = (lax.iota(jnp.int32, length)[None, :] < suf_len[:, None]).astype(jnp.int32)
-        rows = pltpu.VMEM(((requests + 1) * GROUP, HEAD_SIZE), jnp.float32)
-        plan = (xs * cores, LANES)
-        sent = pl.pallas_call(
-            attend_kernel,
-            out_shape=jax.ShapeDtypeStruct((requests, PAD_WIDTH), jnp.bfloat16),
-            in_specs=[smem] * 3 + [vmem] * 6,
-            out_specs=vmem,
-            scratch_shapes=[rows] * 4
-            + [
-                pltpu.VMEM(plan, jnp.int32),
-                pltpu.SMEM(plan, jnp.int32),
+        all_rows = ((requests + 1) * GROUP, HEAD_SIZE)
+        own_rows = (request_count * GROUP, HEAD_SIZE)
+        own = lax.dynamic_slice_in_dim(received, z * request_count, request_count, 0)
+        own_part = jax.ShapeDtypeStruct(own_rows, jnp.float32)
+        plan, heads, *own_parts = pl.pallas_call(
+            local_kernel,
+            out_shape=(
+                jax.ShapeDtypeStruct((xs * cores, LANES), jnp.int32),
+                jax.ShapeDtypeStruct(all_rows, jnp.float32),
+                own_part, own_part, own_part,
+            ),
+            in_specs=[smem] + [vmem] * 4 + [hbm],
+            out_specs=[vmem] * 5,
+            scratch_shapes=[
+                pltpu.VMEM(own_rows, jnp.float32),
+                pltpu.VMEM(suffix_key_value.shape, jnp.bfloat16),
                 pltpu.SemaphoreType.DMA,
             ],
+            compiler_params=pltpu.CompilerParams(vmem_limit_bytes=32 * 1024 * 1024),
+            cost_estimate=pl.CostEstimate(flops=17179869184, bytes_accessed=67108864, transcendentals=1 << 20),
+            name="local_attention",
+        )(
+            held, received, own, fresh_key_value.transpose(1, 0, 2),
+            valid.reshape(-1, 8 * length), suffix_key_value,
+        )
+        sent = pl.pallas_call(
+            prefix_kernel,
+            out_shape=jax.ShapeDtypeStruct((requests, PAD_WIDTH), jnp.bfloat16),
+            in_specs=[smem] * 3 + [vmem] * 4 + [anywhere] * 2,
+            out_specs=vmem,
+            scratch_shapes=[pltpu.VMEM(all_rows, jnp.float32)] * 3
+            + [pltpu.VMEM(near.shape, jnp.bfloat16)] * 2
+            + [pltpu.SemaphoreType.DMA] * 2,
             compiler_params=pltpu.CompilerParams(vmem_limit_bytes=40 * 1024 * 1024),
-            name="attend",
-        )(
-            held, lengths, z[None],
-            received, suffix_key_value, fresh_key_value.transpose(1, 0, 2),
-            valid.reshape(-1, 8 * length), near, far,
-        )
+            name="prefix_attention",
+        )(plan, lengths, z[None], heads, *own_parts, near, far)
     with jax.named_scope("send_parts"):
         parts = exchange(sent.reshape(zs * kvs, rows_each, PAD_WIDTH))
         parts = parts.reshape(zs, kvs, rows_each, PAD_WIDTH)

time: 88.8 us -> 87.4 us (0.984); the launches traced: 88.4 us -> 85.9 us
  blocking collectives: 25.7 us -> 34.5 us
  waiting for transfers between devices: 17 us -> 8.65 us
  local copies, waits for them, and re-layouts: 4.11 us -> 1.98 us
  starting transfers between devices: 30 us -> 28.6 us
  Pallas kernels: 10.8 us -> 11.7 us
    all_to_all x1, waiting for transfers between devices: 17 us -> 0.01 us  [exchange(): lax.all_to_all(slabs, ('z', 'kv'), split_axis=0, concat_axis=0, tiled=True)]
    all_to_all x1, blocking collectives: 25.7 us -> 34.5 us  [exchange(): lax.all_to_all(slabs, ('z', 'kv'), split_axis=0, concat_axis=0, tiled=True)]
    ppermute x3, waiting for transfers between devices: 0.01 us -> 8.64 us  [shards(): lax.ppermute(own_cache, 'x', [(i, i ^ step) for i in range(xs)])]
    ppermute x3, starting transfers between devices: 11.4 us -> 9.96 us  [shards(): lax.ppermute(own_cache, 'x', [(i, i ^ step) for i in range(xs)])]
    unnamed x20 -> x16, local copies, waits for them, and re-layouts: 2.37 us -> 1.33 us
    broadcast_in_dim x2 -> x0, local copies, waits for them, and re-layouts: 1 us -> none  [the longest x1 1 us: shards(): outgoing = jnp.broadcast_to(outgoing[None], (zs,) + outgoing.shape)]
    pallas_call x1 -> x3, Pallas kernels: 8.36 us -> 9.31 us  [the longest x1 4.72 us: shards(): pl.pallas_call(prefix_kernel, out_shape=jax.ShapeDtypeStruct((requests, P...]
  transfers between devices with their start and end apart: 5 -> 5, of which waited for: 1 -> 1; matrix products, arithmetic and copies ran while one was open for 1% -> 1% of each run, Pallas kernels for 0% -> 3%
where the time goes in v3:
time: 87.4 us; the launch traced here: 85.9 us
  blocking collectives  34.5 us (39%)
  starting transfers between devices  28.6 us (33%)
  Pallas kernels  11.7 us (13%)
  waiting for transfers between devices  8.65 us (10%)
  local copies, waits for them, and re-layouts  1.98 us (2%)
    all_to_all x1, blocking collectives, exchange(): lax.all_to_all(slabs, ('z', 'kv'), split_axis=0, concat_axis=0, tiled=True)  34.5 us
    all_to_all x1, starting transfers between devices, exchange(): lax.all_to_all(slabs, ('z', 'kv'), split_axis=0, concat_axis=0, tiled=True)  16.7 us
    ppermute x3, starting transfers between devices, shards(): lax.ppermute(own_cache, 'x', [(i, i ^ step) for i in range(xs)])  9.96 us
    ppermute x3, waiting for transfers between devices, shards(): lax.ppermute(own_cache, 'x', [(i, i ^ step) for i in range(xs)])  8.64 us
    pallas_call x1, Pallas kernels, shards(): pl.pallas_call(prefix_kernel, out_shape=jax.ShapeDtypeStruct((requests, P...  4.72 us
    pallas_call x1, Pallas kernels, shards(): pl.pallas_call(local_kernel, out_shape=(jax.ShapeDtypeStruct((xs * cores,...  2.83 us
    pallas_call x1, Pallas kernels, shards(): pl.pallas_call(combine_kernel, out_shape=jax.ShapeDtypeStruct((rows_each,...  2.4 us
    ppermute x1, starting transfers between devices, shards(): far = lax.ppermute(near, 'core', [(0, 1), (1, 0)])  1.92 us
  transfers between devices with their start and end apart: 5, of which 1 were waited for; matrix products, arithmetic and copies ran while one was open for 1% of the time, Pallas kernels for 3%

profile of v3, /device:TPU:8, one launch (start us, length us, event | category | flops | bytes accessed | tf_op | source)
XLA Modules:
  0.0 85.9 jit_solution(11763938037869679940)
XLA Ops:
  0.0 1.8 %pack_queries.1 = bf16[64,4,1152]{2,1,0:T(4,128)(2,1)} custom-call(s32[1]{0:T(128)} %bitcast.place_ref, s32[3,32]{1,0:T(4,128)} %bitcast.9, s32[64]{0:T(128)} %owner_ref.1, bf16[4,8192]{1,0:T(4,128)(2,1)} %query_ref.1), custom_call_target="tpu_custom_call" | custom-call | tf_op jit(solution)/shard_map/send_queries/pack_queries/pallas_call | solution.py:323
  1.8 16.7 %all-to-all-start = ((bf16[64,4,1152]{2,1,0:T(4,128)(2,1)}), bf16[64,4,1152]{2,1,0:T(4,128)(2,1)S(1)}, u32[]{:S(2)}, u32[]{:S(2)}) async-start(bf16[64,4,1152]{2,1,0:T(4,128)(2,1)} %pack_queries.1), calls=%async_computation | async-start | bytes 1179648 | tf_op jit(solution)/shard_map/send_queries/all_to_all | solution.py:320
  18.5 3.4 %collective-permute-start = (bf16[1,2,512,128]{3,2,1,0:T(8,128)(2,1)S(1)}, bf16[1,2,512,128]{3,2,1,0:T(8,128)(2,1)S(1)}, u32[]{:S(2)}, u32[]{:S(2)}) collective-permute-start(bf16[1,2,512,128]{3,2,1,0:T(8,128)(2,1)S(1)} %copy-done.1), channel_id=1, source_target_pairs={{0,128},{128,0},{256,384},{384,256},{1,129},{129,1},{257,385},{385... | collective-permute-start | bytes 786440 | tf_op jit(solution)/shard_map/send_prefix/ppermute | solution.py:334
  21.9 4.0 %collective-permute-start.1 = (bf16[1,2,512,128]{3,2,1,0:T(8,128)(2,1)S(1)}, bf16[1,2,512,128]{3,2,1,0:T(8,128)(2,1)S(1)}, u32[]{:S(2)}, u32[]{:S(2)}) collective-permute-start(bf16[1,2,512,128]{3,2,1,0:T(8,128)(2,1)S(1)} %copy-done.1), channel_id=1, source_target_pairs={{0,384},{128,256},{256,128},{384,0},{1,385},{129,257},{257,129},{3... | collective-permute-start | bytes 786440 | tf_op jit(solution)/shard_map/send_prefix/ppermute | solution.py:334
  25.9 2.6 %collective-permute-start.2 = (bf16[1,2,512,128]{3,2,1,0:T(8,128)(2,1)S(1)}, bf16[1,2,512,128]{3,2,1,0:T(8,128)(2,1)S(1)}, u32[]{:S(2)}, u32[]{:S(2)}) collective-permute-start(bf16[1,2,512,128]{3,2,1,0:T(8,128)(2,1)S(1)} %copy-done.1), channel_id=1, source_target_pairs={{0,256},{128,384},{256,0},{384,128},{1,257},{129,385},{257,1},{385... | collective-permute-start | bytes 786440 | tf_op jit(solution)/shard_map/send_prefix/ppermute | solution.py:334
  28.5 0.1 lt.29
  28.6 0.1 lt.30
  28.7 0.1 lt.31
  28.7 0.1 lt.27
  28.9 0.1 pad_add_fusion.held_ref
  28.9 0.2 select_reduce_fusion.length_ref
  29.1 0.0 collective-permute-done
  29.2 8.6 %collective-permute-done.1 = bf16[1,2,512,128]{3,2,1,0:T(8,128)(2,1)S(1)} collective-permute-done((bf16[1,2,512,128]{3,2,1,0:T(8,128)(2,1)S(1)}, bf16[1,2,512,128]{3,2,1,0:T(8,128)(2,1)S(1)}, u32[]{:S(2)}, u32[]{:S(2)}) %collective-permute-start.1) | collective-permute-done | bytes 262176 | tf_op jit(solution)/shard_map/send_prefix/ppermute | solution.py:334
  37.9 0.0 collective-permute-done.2
  37.9 1.9 %collective-permute-start.3 = (bf16[4,2,512,128]{3,2,1,0:T(8,128)(2,1)S(1)}, bf16[4,2,512,128]{3,2,1,0:T(8,128)(2,1)S(1)}, u32[]{:S(2)}, u32[]{:S(2)}) collective-permute-start(bf16[4,2,512,128]{3,2,1,0:T(8,128)(2,1)S(1)} %constant_dynamic-update-slice_fusion.near_ref), channel_id=1, source_target_pairs={{0,8},{8,0},{1,9},{9,1},{2,10},{10,2},{3,11},{11,3},{4,12},{12,4},... | collective-permute-start | bytes 3145736 | tf_op jit(solution)/shard_map/send_prefix/ppermute | solution.py:336
  39.9 0.1 reshape.16.query_ref
  40.0 0.0 copy-start
  40.0 1.2 %copy-done = bf16[32,2,64,128]{3,2,1,0:T(8,128)(2,1)S(1)} copy-done((bf16[32,2,64,128]{3,2,1,0:T(8,128)(2,1)S(1)}, bf16[32,2,64,128]{3,2,1,0:T(8,128)(2,1)}, u32[]{:S(2)}) %copy-start) | copy-done | bytes 1048600
  41.3 2.8 %local_attention.1 = (s32[8,128]{1,0:T(8,128)S(1)}, f32[2056,128]{1,0:T(8,128)S(1)}, f32[256,128]{1,0:T(8,128)S(1)}, f32[256,128]{1,0:T(8,128)S(1)}, f32[256,128]{1,0:T(8,128)S(1)}) custom-call(s32[8]{0:T(128)S(1)} %pad_add_fusion.held_ref, bf16[256,1152]{1,0:T(8,128)(2,1)S(1)} %reshape.16.query_ref, ...), custom_call_target="tpu_custom_call" | custom-call | flops 17179869184 | bytes 67108864 | tf_op jit(solution)/shard_map/attend/local_attention/pallas_call | solution.py:351
  44.1 0.0 collective-permute-done.3.far_ref
  44.1 4.7 %prefix_attention.1 = bf16[256,1152]{1,0:T(8,128)(2,1)S(1)} custom-call(s32[8,128]{1,0:T(8,128)S(1)} %get-tuple-element.13.plan_ref, s32[8]{0:T(128)S(1)} %select_reduce_fusion.length_ref, s32[1]{0:T(128)} %bitcast.3.place_ref, f32[2056,128]{1,0:T(8,128)S(1)} %get-tuple-element.14.heads_ref, f32[256,128]{1,0:T(8,128)S(1)} %get-tuple-element.15.own_out, ...), custom_call_target="tpu_custom_call" | custom-call | tf_op jit(solution)/shard_map/attend/prefix_attention/pallas_call | solution.py:372
  48.8 0.1 reshape.17
  49.0 34.5 %all_to_all.10 = bf16[64,4,1152]{2,1,0:T(4,128)(2,1)S(1)} all-to-all(bf16[64,4,1152]{2,1,0:T(4,128)(2,1)S(1)} %reshape.17), channel_id=1, replica_groups=mesh['x'=4,'z'=8,'core'=2,'kv'=8] {'z','kv'}, dimensions={0} | all-to-all | bytes 1179648 | tf_op jit(solution)/shard_map/send_parts/all_to_all | solution.py:320
  83.5 2.4 %combine.1 = bf16[4,8192]{1,0:T(4,128)(2,1)} custom-call(bf16[8,8,4,1152]{3,2,1,0:T(4,128)(2,1)S(1)} %bitcast.7), custom_call_target="tpu_custom_call" | custom-call | tf_op jit(solution)/shard_map/combine/combine/pallas_call | solution.py:387
  (20 shorter events, 0.2 us)
Async XLA Ops:
  0.0 28.8 %copy-start.4 = (s32[4]{0:T(128)S(1)}, s32[4]{0:T(128)}, u32[]{:S(2)}) copy-start(s32[4]{0:T(128)} %constant.31.clone) | copy-start | bytes 52
  0.0 18.5 %copy-start.1 = (bf16[1,2,512,128]{3,2,1,0:T(8,128)(2,1)S(1)}, bf16[1,2,512,128]{3,2,1,0:T(8,128)(2,1)}, u32[]{:S(2)}) copy-start(bf16[1,2,512,128]{3,2,1,0:T(8,128)(2,1)} %param.14) | copy-start | bytes 786436
  0.0 28.5 %copy-start.3 = (s32[32]{0:T(128)S(1)}, s32[32]{0:T(128)}, u32[]{:S(2)}) copy-start(s32[32]{0:T(128)} %param.13) | copy-start | bytes 388
  1.8 27.2 %copy-start.5 = (s32[64]{0:T(128)S(1)}, s32[64]{0:T(128)}, u32[]{:S(2)}) copy-start(s32[64]{0:T(128)} %param.12) | copy-start | bytes 772
  1.8 27.4 %copy-start.2 = (bf16[32,2,128]{2,1,0:T(2,128)(2,1)S(1)}, bf16[32,2,128]{2,1,0:T(2,128)(2,1)}, u32[]{:S(2)}) copy-start(bf16[32,2,128]{2,1,0:T(2,128)(2,1)} %param.16) | copy-start | bytes 49156
  1.8 38.1 %all-to-all-start = ((bf16[64,4,1152]{2,1,0:T(4,128)(2,1)}), bf16[64,4,1152]{2,1,0:T(4,128)(2,1)S(1)}, u32[]{:S(2)}, u32[]{:S(2)}) async-start(bf16[64,4,1152]{2,1,0:T(4,128)(2,1)} %pack_queries.1), calls=%async_computation | async-start | bytes 1179648 | tf_op jit(solution)/shard_map/send_queries/all_to_all | solution.py:320
  18.5 10.6 %collective-permute-start = (bf16[1,2,512,128]{3,2,1,0:T(8,128)(2,1)S(1)}, bf16[1,2,512,128]{3,2,1,0:T(8,128)(2,1)S(1)}, u32[]{:S(2)}, u32[]{:S(2)}) collective-permute-start(bf16[1,2,512,128]{3,2,1,0:T(8,128)(2,1)S(1)} %copy-done.1), channel_id=1, source_target_pairs={{0,128},{128,0},{256,384},{384,256},{1,129},{129,1},{257,385},{385... | collective-permute-start | bytes 786440 | tf_op jit(solution)/shard_map/send_prefix/ppermute | solution.py:334
  21.9 15.9 %collective-permute-start.1 = (bf16[1,2,512,128]{3,2,1,0:T(8,128)(2,1)S(1)}, bf16[1,2,512,128]{3,2,1,0:T(8,128)(2,1)S(1)}, u32[]{:S(2)}, u32[]{:S(2)}) collective-permute-start(bf16[1,2,512,128]{3,2,1,0:T(8,128)(2,1)S(1)} %copy-done.1), channel_id=1, source_target_pairs={{0,384},{128,256},{256,128},{384,0},{1,385},{129,257},{257,129},{3... | collective-permute-start | bytes 786440 | tf_op jit(solution)/shard_map/send_prefix/ppermute | solution.py:334
  25.9 12.0 %collective-permute-start.2 = (bf16[1,2,512,128]{3,2,1,0:T(8,128)(2,1)S(1)}, bf16[1,2,512,128]{3,2,1,0:T(8,128)(2,1)S(1)}, u32[]{:S(2)}, u32[]{:S(2)}) collective-permute-start(bf16[1,2,512,128]{3,2,1,0:T(8,128)(2,1)S(1)} %copy-done.1), channel_id=1, source_target_pairs={{0,256},{128,384},{256,0},{384,128},{1,257},{129,385},{257,1},{385... | collective-permute-start | bytes 786440 | tf_op jit(solution)/shard_map/send_prefix/ppermute | solution.py:334
  37.9 6.2 %collective-permute-start.3 = (bf16[4,2,512,128]{3,2,1,0:T(8,128)(2,1)S(1)}, bf16[4,2,512,128]{3,2,1,0:T(8,128)(2,1)S(1)}, u32[]{:S(2)}, u32[]{:S(2)}) collective-permute-start(bf16[4,2,512,128]{3,2,1,0:T(8,128)(2,1)S(1)} %constant_dynamic-update-slice_fusion.near_ref), channel_id=1, source_target_pairs={{0,8},{8,0},{1,9},{9,1},{2,10},{10,2},{3,11},{11,3},{4,12},{12,4},... | collective-permute-start | bytes 3145736 | tf_op jit(solution)/shard_map/send_prefix/ppermute | solution.py:336
  40.0 1.2 %copy-start = (bf16[32,2,64,128]{3,2,1,0:T(8,128)(2,1)S(1)}, bf16[32,2,64,128]{3,2,1,0:T(8,128)(2,1)}, u32[]{:S(2)}) copy-start(bf16[32,2,64,128]{3,2,1,0:T(8,128)(2,1)} %stored_ref.1) | copy-start | bytes 3145732

commit v4 on v3

--- a/solution.py
+++ b/solution.py
@@ -214,23 +214,21 @@
             sent_ref[copy * heads_kv + group, :, WIDTH:] = tail
 
 
-def local_kernel(
-    held_ref, query_ref, own_ref, fresh_ref, valid_ref, stored_ref,
-    plan_ref, heads_ref, acc, high, total,
-    own_heads_ref, suffix_ref, suffix_sem,
-):
-    fetch = pltpu.make_async_copy(stored_ref, suffix_ref, suffix_sem)
-    fetch.start()
+def plan_kernel(held_ref, query_ref, plan_ref, heads_ref):
     requests = query_ref.shape[0]
     make_plan(held_ref, query_ref[:, WIDTH:].astype(jnp.float32), plan_ref)
     for head in range(GROUP):
-        columns = slice(head * HEAD_SIZE, (head + 1) * HEAD_SIZE)
-        part = query_ref[:, columns].astype(jnp.float32)
+        part = query_ref[:, head * HEAD_SIZE : (head + 1) * HEAD_SIZE].astype(jnp.float32)
         heads_ref[pl.ds(head, requests, stride=GROUP), :] = part
-        part = own_ref[:, columns].astype(jnp.float32)
+    heads_ref[requests * GROUP :, :] = jnp.zeros((GROUP, HEAD_SIZE), jnp.float32)
+
+
+def local_kernel(
+    own_ref, fresh_ref, valid_ref, suffix_ref, acc, high, total, own_heads_ref
+):
+    for head in range(GROUP):
+        part = own_ref[:, head * HEAD_SIZE : (head + 1) * HEAD_SIZE].astype(jnp.float32)
         own_heads_ref[pl.ds(head, own_ref.shape[0], stride=GROUP), :] = part
-    heads_ref[requests * GROUP :, :] = jnp.zeros((GROUP, HEAD_SIZE), jnp.float32)
-    fetch.wait()
     suffix_part(0, suffix_ref, fresh_ref, valid_ref, own_heads_ref, acc, high, total)
 
 
@@ -314,7 +312,6 @@
     smem = pl.BlockSpec(memory_space=pltpu.SMEM)
     vmem = pl.BlockSpec(memory_space=pltpu.VMEM)
     anywhere = pl.BlockSpec(memory_space=pl.ANY)
-    hbm = pl.BlockSpec(memory_space=pltpu.HBM)
 
     def exchange(slabs):
         return lax.all_to_all(slabs, ("z", "kv"), split_axis=0, concat_axis=0, tiled=True)
@@ -348,26 +345,32 @@
         own_rows = (request_count * GROUP, HEAD_SIZE)
         own = lax.dynamic_slice_in_dim(received, z * request_count, request_count, 0)
         own_part = jax.ShapeDtypeStruct(own_rows, jnp.float32)
-        plan, heads, *own_parts = pl.pallas_call(
-            local_kernel,
+        plan, heads = pl.pallas_call(
+            plan_kernel,
             out_shape=(
                 jax.ShapeDtypeStruct((xs * cores, LANES), jnp.int32),
                 jax.ShapeDtypeStruct(all_rows, jnp.float32),
-                own_part, own_part, own_part,
             ),
-            in_specs=[smem] + [vmem] * 4 + [hbm],
-            out_specs=[vmem] * 5,
-            scratch_shapes=[
-                pltpu.VMEM(own_rows, jnp.float32),
-                pltpu.VMEM(suffix_key_value.shape, jnp.bfloat16),
-                pltpu.SemaphoreType.DMA,
-            ],
+            in_specs=[smem, vmem],
+            out_specs=[vmem] * 2,
+            cost_estimate=pl.CostEstimate(
+                flops=1 << 34, bytes_accessed=1 << 22, transcendentals=0
+            ),
             compiler_params=pltpu.CompilerParams(vmem_limit_bytes=32 * 1024 * 1024),
-            cost_estimate=pl.CostEstimate(flops=17179869184, bytes_accessed=67108864, transcendentals=1 << 20),
+            name="plan_requests",
+        )(held, received)
+        plan, own = lax.optimization_barrier((plan, own))
+        own_parts = pl.pallas_call(
+            local_kernel,
+            out_shape=(own_part, own_part, own_part),
+            in_specs=[vmem] * 4,
+            out_specs=[vmem] * 3,
+            scratch_shapes=[pltpu.VMEM(own_rows, jnp.float32)],
+            compiler_params=pltpu.CompilerParams(vmem_limit_bytes=32 * 1024 * 1024),
             name="local_attention",
         )(
-            held, received, own, fresh_key_value.transpose(1, 0, 2),
-            valid.reshape(-1, 8 * length), suffix_key_value,
+            own, fresh_key_value.transpose(1, 0, 2), valid.reshape(-1, 8 * length),
+            suffix_key_value,
         )
         sent = pl.pallas_call(
             prefix_kernel,

time: 87.4 us -> 85.2 us (0.975)
  blocking collectives: 34.5 us -> 33 us
  local copies, waits for them, and re-layouts: 1.98 us -> 0.76 us
    all_to_all x1, blocking collectives: 34.5 us -> 33 us  [exchange(): lax.all_to_all(slabs, ('z', 'kv'), split_axis=0, concat_axis=0, tiled=True)]
    unnamed x16, local copies, waits for them, and re-layouts: 1.33 us -> 0.12 us
    pallas_call x1, Pallas kernels: 4.72 us -> 5.6 us  [shards(): pl.pallas_call(prefix_kernel, out_shape=jax.ShapeDtypeStruct((requests, P...]
    pallas_call x1 -> x2, Pallas kernels: 2.83 us -> 2.73 us  [the longest x1 1.5 us: shards(): pl.pallas_call(plan_kernel, out_shape=(jax.ShapeDtypeStruct((xs * cores,...]
where the time goes in v4:
time: 85.2 us; the launch traced here: 84 us
  blocking collectives  33 us (39%)
  starting transfers between devices  28.6 us (34%)
  Pallas kernels  12.5 us (15%)
  waiting for transfers between devices  8.65 us (10%)
    all_to_all x1, blocking collectives, exchange(): lax.all_to_all(slabs, ('z', 'kv'), split_axis=0, concat_axis=0, tiled=True)  33 us
    all_to_all x1, starting transfers between devices, exchange(): lax.all_to_all(slabs, ('z', 'kv'), split_axis=0, concat_axis=0, tiled=True)  16.7 us
    ppermute x3, starting transfers between devices, shards(): lax.ppermute(own_cache, 'x', [(i, i ^ step) for i in range(xs)])  9.96 us
    ppermute x3, waiting for transfers between devices, shards(): lax.ppermute(own_cache, 'x', [(i, i ^ step) for i in range(xs)])  8.64 us
    pallas_call x1, Pallas kernels, shards(): pl.pallas_call(prefix_kernel, out_shape=jax.ShapeDtypeStruct((requests, P...  5.6 us
    pallas_call x1, Pallas kernels, shards(): pl.pallas_call(combine_kernel, out_shape=jax.ShapeDtypeStruct((rows_each,...  2.4 us
    ppermute x1, starting transfers between devices, shards(): far = lax.ppermute(near, 'core', [(0, 1), (1, 0)])  1.92 us
    pallas_call x1, Pallas kernels, shards(): pl.pallas_call(pack_kernel, out_shape=jax.ShapeDtypeStruct((zs * kvs, row...  1.77 us
  transfers between devices with their start and end apart: 5, of which 1 were waited for; matrix products, arithmetic and copies ran while one was open for 1% of the time, Pallas kernels for 3%

profile of v4, /device:TPU:8, one launch (start us, length us, event | category | flops | bytes accessed | tf_op | source)
XLA Modules:
  0.0 84.0 jit_solution(16590979773078447126)
XLA Ops:
  0.0 1.8 %pack_queries.1 = bf16[64,4,1152]{2,1,0:T(4,128)(2,1)} custom-call(s32[1]{0:T(128)} %bitcast.place_ref, s32[3,32]{1,0:T(4,128)} %bitcast.9, s32[64]{0:T(128)} %owner_ref.1, bf16[4,8192]{1,0:T(4,128)(2,1)} %query_ref.1), custom_call_target="tpu_custom_call" | custom-call | tf_op jit(solution)/shard_map/send_queries/pack_queries/pallas_call | solution.py:320
  1.8 16.7 %all-to-all-start = ((bf16[64,4,1152]{2,1,0:T(4,128)(2,1)}), bf16[64,4,1152]{2,1,0:T(4,128)(2,1)S(1)}, u32[]{:S(2)}, u32[]{:S(2)}) async-start(bf16[64,4,1152]{2,1,0:T(4,128)(2,1)} %pack_queries.1), calls=%async_computation | async-start | bytes 1179648 | tf_op jit(solution)/shard_map/send_queries/all_to_all | solution.py:317
  18.5 3.4 %collective-permute-start = (bf16[1,2,512,128]{3,2,1,0:T(8,128)(2,1)S(1)}, bf16[1,2,512,128]{3,2,1,0:T(8,128)(2,1)S(1)}, u32[]{:S(2)}, u32[]{:S(2)}) collective-permute-start(bf16[1,2,512,128]{3,2,1,0:T(8,128)(2,1)S(1)} %copy-done.1), channel_id=1, source_target_pairs={{0,128},{128,0},{256,384},{384,256},{1,129},{129,1},{257,385},{385... | collective-permute-start | bytes 786440 | tf_op jit(solution)/shard_map/send_prefix/ppermute | solution.py:331
  21.9 4.0 %collective-permute-start.1 = (bf16[1,2,512,128]{3,2,1,0:T(8,128)(2,1)S(1)}, bf16[1,2,512,128]{3,2,1,0:T(8,128)(2,1)S(1)}, u32[]{:S(2)}, u32[]{:S(2)}) collective-permute-start(bf16[1,2,512,128]{3,2,1,0:T(8,128)(2,1)S(1)} %copy-done.1), channel_id=1, source_target_pairs={{0,384},{128,256},{256,128},{384,0},{1,385},{129,257},{257,129},{3... | collective-permute-start | bytes 786440 | tf_op jit(solution)/shard_map/send_prefix/ppermute | solution.py:331
  25.9 2.6 %collective-permute-start.2 = (bf16[1,2,512,128]{3,2,1,0:T(8,128)(2,1)S(1)}, bf16[1,2,512,128]{3,2,1,0:T(8,128)(2,1)S(1)}, u32[]{:S(2)}, u32[]{:S(2)}) collective-permute-start(bf16[1,2,512,128]{3,2,1,0:T(8,128)(2,1)S(1)} %copy-done.1), channel_id=1, source_target_pairs={{0,256},{128,384},{256,0},{384,128},{1,257},{129,385},{257,1},{385... | collective-permute-start | bytes 786440 | tf_op jit(solution)/shard_map/send_prefix/ppermute | solution.py:331
  28.5 0.1 lt.29
  28.6 0.1 lt.30
  28.7 0.1 lt.31
  28.8 0.1 lt.27
  28.9 0.1 pad_add_fusion.held_ref
  29.0 0.2 select_reduce_fusion.length_ref
  29.2 0.0 collective-permute-done
  29.2 8.6 %collective-permute-done.1 = bf16[1,2,512,128]{3,2,1,0:T(8,128)(2,1)S(1)} collective-permute-done((bf16[1,2,512,128]{3,2,1,0:T(8,128)(2,1)S(1)}, bf16[1,2,512,128]{3,2,1,0:T(8,128)(2,1)S(1)}, u32[]{:S(2)}, u32[]{:S(2)}) %collective-permute-start.1) | collective-permute-done | bytes 262176 | tf_op jit(solution)/shard_map/send_prefix/ppermute | solution.py:331
  37.9 0.0 collective-permute-done.2
  37.9 1.9 %collective-permute-start.3 = (bf16[4,2,512,128]{3,2,1,0:T(8,128)(2,1)S(1)}, bf16[4,2,512,128]{3,2,1,0:T(8,128)(2,1)S(1)}, u32[]{:S(2)}, u32[]{:S(2)}) collective-permute-start(bf16[4,2,512,128]{3,2,1,0:T(8,128)(2,1)S(1)} %constant_dynamic-update-slice_fusion.near_ref), channel_id=1, source_target_pairs={{0,8},{8,0},{1,9},{9,1},{2,10},{10,2},{3,11},{11,3},{4,12},{12,4},... | collective-permute-start | bytes 3145736 | tf_op jit(solution)/shard_map/send_prefix/ppermute | solution.py:333
  39.9 0.1 reshape.16.query_ref
  40.0 0.0 copy-start
  40.1 1.5 %plan_requests.1 = (s32[8,128]{1,0:T(8,128)S(1)}, f32[2056,128]{1,0:T(8,128)S(1)}) custom-call(s32[8]{0:T(128)S(1)} %pad_add_fusion.held_ref, bf16[256,1152]{1,0:T(8,128)(2,1)S(1)} %reshape.16.query_ref), custom_call_target="tpu_custom_call" | custom-call | flops 17179869184 | bytes 4194304 | tf_op jit(solution)/shard_map/attend/plan_requests/pallas_call | solution.py:348
  41.6 1.2 %local_attention.1 = (f32[256,128]{1,0:T(8,128)S(1)}, f32[256,128]{1,0:T(8,128)S(1)}, f32[256,128]{1,0:T(8,128)S(1)}) custom-call(bf16[32,1152]{1,0:T(8,128)(2,1)S(1)} %constant_dynamic-slice_fusion.own_ref, bf16[2,32,128]{2,1,0:T(8,128)(2,1)S(1)} %bitcast.8, s32[4,512]{1,0:T(4,128)S(1)} %compare_convert_fusion.valid_ref, bf16[32,2,64,128]{3,2,1,0:T(8,128)(2,1)S(1)} %copy-done), custom_call_target="tpu_custom_call" | custom-call | tf_op jit(solution)/shard_map/attend/local_attention/pallas_call | solution.py:363
  42.8 0.0 collective-permute-done.3.far_ref
  42.8 5.6 %prefix_attention.1 = bf16[256,1152]{1,0:T(8,128)(2,1)S(1)} custom-call(s32[8,128]{1,0:T(8,128)S(1)} %get-tuple-element.16.plan_ref, s32[8]{0:T(128)S(1)} %select_reduce_fusion.length_ref, s32[1]{0:T(128)} %bitcast.2.place_ref, f32[2056,128]{1,0:T(8,128)S(1)} %get-tuple-element.17.heads_ref, f32[256,128]{1,0:T(8,128)S(1)} %get-tuple-element.19.own_out, ...), custom_call_target="tpu_custom_call" | custom-call | tf_op jit(solution)/shard_map/attend/prefix_attention/pallas_call | solution.py:375
  48.4 0.1 reshape.17
  48.6 33.0 %all_to_all.10 = bf16[64,4,1152]{2,1,0:T(4,128)(2,1)S(1)} all-to-all(bf16[64,4,1152]{2,1,0:T(4,128)(2,1)S(1)} %reshape.17), channel_id=1, replica_groups=mesh['x'=4,'z'=8,'core'=2,'kv'=8] {'z','kv'}, dimensions={0} | all-to-all | bytes 1179648 | tf_op jit(solution)/shard_map/send_parts/all_to_all | solution.py:317
  81.6 2.4 %combine.1 = bf16[4,8192]{1,0:T(4,128)(2,1)} custom-call(bf16[8,8,4,1152]{3,2,1,0:T(4,128)(2,1)S(1)} %bitcast.7), custom_call_target="tpu_custom_call" | custom-call | tf_op jit(solution)/shard_map/combine/combine/pallas_call | solution.py:390
  (21 shorter events, 0.2 us)
Async XLA Ops:
  0.0 28.8 %copy-start.4 = (s32[4]{0:T(128)S(1)}, s32[4]{0:T(128)}, u32[]{:S(2)}) copy-start(s32[4]{0:T(128)} %constant.31.clone) | copy-start | bytes 52
  0.0 18.5 %copy-start.1 = (bf16[1,2,512,128]{3,2,1,0:T(8,128)(2,1)S(1)}, bf16[1,2,512,128]{3,2,1,0:T(8,128)(2,1)}, u32[]{:S(2)}) copy-start(bf16[1,2,512,128]{3,2,1,0:T(8,128)(2,1)} %param.14) | copy-start | bytes 786436
  0.0 28.5 %copy-start.3 = (s32[32]{0:T(128)S(1)}, s32[32]{0:T(128)}, u32[]{:S(2)}) copy-start(s32[32]{0:T(128)} %param.13) | copy-start | bytes 388
  1.8 27.2 %copy-start.5 = (s32[64]{0:T(128)S(1)}, s32[64]{0:T(128)}, u32[]{:S(2)}) copy-start(s32[64]{0:T(128)} %param.12) | copy-start | bytes 772
  1.8 27.4 %copy-start.2 = (bf16[32,2,128]{2,1,0:T(2,128)(2,1)S(1)}, bf16[32,2,128]{2,1,0:T(2,128)(2,1)}, u32[]{:S(2)}) copy-start(bf16[32,2,128]{2,1,0:T(2,128)(2,1)} %param.16) | copy-start | bytes 49156
  1.8 38.1 %all-to-all-start = ((bf16[64,4,1152]{2,1,0:T(4,128)(2,1)}), bf16[64,4,1152]{2,1,0:T(4,128)(2,1)S(1)}, u32[]{:S(2)}, u32[]{:S(2)}) async-start(bf16[64,4,1152]{2,1,0:T(4,128)(2,1)} %pack_queries.1), calls=%async_computation | async-start | bytes 1179648 | tf_op jit(solution)/shard_map/send_queries/all_to_all | solution.py:317
  18.5 10.6 %collective-permute-start = (bf16[1,2,512,128]{3,2,1,0:T(8,128)(2,1)S(1)}, bf16[1,2,512,128]{3,2,1,0:T(8,128)(2,1)S(1)}, u32[]{:S(2)}, u32[]{:S(2)}) collective-permute-start(bf16[1,2,512,128]{3,2,1,0:T(8,128)(2,1)S(1)} %copy-done.1), channel_id=1, source_target_pairs={{0,128},{128,0},{256,384},{384,256},{1,129},{129,1},{257,385},{385... | collective-permute-start | bytes 786440 | tf_op jit(solution)/shard_map/send_prefix/ppermute | solution.py:331
  21.9 15.9 %collective-permute-start.1 = (bf16[1,2,512,128]{3,2,1,0:T(8,128)(2,1)S(1)}, bf16[1,2,512,128]{3,2,1,0:T(8,128)(2,1)S(1)}, u32[]{:S(2)}, u32[]{:S(2)}) collective-permute-start(bf16[1,2,512,128]{3,2,1,0:T(8,128)(2,1)S(1)} %copy-done.1), channel_id=1, source_target_pairs={{0,384},{128,256},{256,128},{384,0},{1,385},{129,257},{257,129},{3... | collective-permute-start | bytes 786440 | tf_op jit(solution)/shard_map/send_prefix/ppermute | solution.py:331
  25.9 12.0 %collective-permute-start.2 = (bf16[1,2,512,128]{3,2,1,0:T(8,128)(2,1)S(1)}, bf16[1,2,512,128]{3,2,1,0:T(8,128)(2,1)S(1)}, u32[]{:S(2)}, u32[]{:S(2)}) collective-permute-start(bf16[1,2,512,128]{3,2,1,0:T(8,128)(2,1)S(1)} %copy-done.1), channel_id=1, source_target_pairs={{0,256},{128,384},{256,0},{384,128},{1,257},{129,385},{257,1},{385... | collective-permute-start | bytes 786440 | tf_op jit(solution)/shard_map/send_prefix/ppermute | solution.py:331
  37.9 4.9 %collective-permute-start.3 = (bf16[4,2,512,128]{3,2,1,0:T(8,128)(2,1)S(1)}, bf16[4,2,512,128]{3,2,1,0:T(8,128)(2,1)S(1)}, u32[]{:S(2)}, u32[]{:S(2)}) collective-permute-start(bf16[4,2,512,128]{3,2,1,0:T(8,128)(2,1)S(1)} %constant_dynamic-update-slice_fusion.near_ref), channel_id=1, source_target_pairs={{0,8},{8,0},{1,9},{9,1},{2,10},{10,2},{3,11},{11,3},{4,12},{12,4},... | collective-permute-start | bytes 3145736 | tf_op jit(solution)/shard_map/send_prefix/ppermute | solution.py:333
  40.0 1.5 %copy-start = (bf16[32,2,64,128]{3,2,1,0:T(8,128)(2,1)S(1)}, bf16[32,2,64,128]{3,2,1,0:T(8,128)(2,1)}, u32[]{:S(2)}) copy-start(bf16[32,2,64,128]{3,2,1,0:T(8,128)(2,1)} %suffix_ref.1) | copy-start | bytes 3145732
